TPU v7x, 32 devices: a whole 2x2x4 slice. The times are simulated.
32 devices in a mesh: dp: 4 (over z), row: 2 (over core), col: 4 (over y, x).
Axes of the slice: x: 2, y: 2, z: 4, core: 2. Of those that a mesh axis runs over, the one named last changes fastest.
Arguments:
- inputs: bfloat16 [2048, 2048], P('dp', ('row', 'col')), may hold values from -11 to 11
- segments: int32 [2048], replicated, may hold values from 0 to 3, as said below
- cotangent: bfloat16 [2048, 2048], P('dp', ('row', 'col')), may hold values from -6 to 6
- w_qkv: float32 [2, 1024, 4, 640], P('row', 'dp', 'col'), may hold values from -0.1875 to 0.1875
- w_out: float32 [4, 512, 2048], P('col', 'dp', 'row'), may hold values from -0.5 to 0.5
- w_gate_up: float32 [2, 1024, 2, 5632], P('row', 'dp', None, 'col'), may hold values from -0.125 to 0.125
- w_down: float32 [4, 1408, 2048], P('col', 'dp', 'row'), may hold values from -0.078125 to 0.078125
- gains: float32 [2, 8, 256], P(None, ('row', 'col'), 'dp'), may hold values from 0.5 to 1.5
- first_qkv: float32 [2, 1024, 4, 640], P('row', 'dp', 'col'), may hold values from -29.86819 to 29.86819
- second_qkv: float32 [2, 1024, 4, 640], P('row', 'dp', 'col'), may hold values from 108.544 to 430.08
- first_out: float32 [4, 512, 2048], P('col', 'dp', 'row'), may hold values from -6.788225 to 6.788225
- second_out: float32 [4, 512, 2048], P('col', 'dp', 'row'), may hold values from 3.584 to 35.84
- first_gate_up: float32 [2, 1024, 2, 5632], P('row', 'dp', None, 'col'), may hold values from -10.589631 to 10.589631
- second_gate_up: float32 [2, 1024, 2, 5632], P('row', 'dp', None, 'col'), may hold values from 13.312 to 53.248
- first_down: float32 [4, 1408, 2048], P('col', 'dp', 'row'), may hold values from -17.920914 to 17.920914
- second_down: float32 [4, 1408, 2048], P('col', 'dp', 'row'), may hold values from 38.912 to 155.648
- first_gains: float32 [2, 8, 256], P(None, ('row', 'col'), 'dp'), may hold values from -29.86819 to 29.86819
- second_gains: float32 [2, 8, 256], P(None, ('row', 'col'), 'dp'), may hold values from 32.768 to 327.68
Outputs:
- layer_output: bfloat16 [2048, 2048], P('dp', ('row', 'col'))
- input_grad: float32 [2048, 2048], P('dp', ('row', 'col'))
- grad_qkv: float32 [2, 1024, 4, 640], P('row', 'dp', 'col')
- new_first_qkv: float32 [2, 1024, 4, 640], P('row', 'dp', 'col')
- new_second_qkv: float32 [2, 1024, 4, 640], P('row', 'dp', 'col')
- new_qkv: float32 [2, 1024, 4, 640], P('row', 'dp', 'col')
- grad_out: float32 [4, 512, 2048], P('col', 'dp', 'row')
- new_first_out: float32 [4, 512, 2048], P('col', 'dp', 'row')
- new_second_out: float32 [4, 512, 2048], P('col', 'dp', 'row')
- new_out: float32 [4, 512, 2048], P('col', 'dp', 'row')
- grad_gate_up: float32 [2, 1024, 2, 5632], P('row', 'dp', None, 'col')
- new_first_gate_up: float32 [2, 1024, 2, 5632], P('row', 'dp', None, 'col')
- new_second_gate_up: float32 [2, 1024, 2, 5632], P('row', 'dp', None, 'col')
- new_gate_up: float32 [2, 1024, 2, 5632], P('row', 'dp', None, 'col')
- grad_down: float32 [4, 1408, 2048], P('col', 'dp', 'row')
- new_first_down: float32 [4, 1408, 2048], P('col', 'dp', 'row')
- new_second_down: float32 [4, 1408, 2048], P('col', 'dp', 'row')
- new_down: float32 [4, 1408, 2048], P('col', 'dp', 'row')
- grad_gains: float32 [2, 8, 256], P(None, ('row', 'col'), 'dp')
- new_first_gains: float32 [2, 8, 256], P(None, ('row', 'col'), 'dp')
- new_second_gains: float32 [2, 8, 256], P(None, ('row', 'col'), 'dp')
- new_gains: float32 [2, 8, 256], P(None, ('row', 'col'), 'dp')
Inputs may be any that keep to these rules, and one draw needn't show every extreme that they name: `segments`: segment numbers start at 0, never fall along the tokens and skip no number; each number is one document, whose tokens are consecutive and lie within one sequence of 2048 tokens; every sequence holds exactly 4 documents, one of which begins within its first 512 tokens and ends within its last 512 tokens.
All inputs are finite; a program needn't handle non-finite values.
Results may differ from a plain program's by a relative error of at most 0.017.
The roundings to bfloat16 on the way count: a program that leaves them out, or rounds other values in their place, can miss the bound.
Values may be sent and summed in bfloat16 or wider, within the bound.
A program may use at most 192 MiB of HBM per device.

v0:
```python
import jax
import jax.numpy as jnp
from jax import lax
from jax.sharding import PartitionSpec as P

D = 2048
HD = 64
SEQ = 4096
STEP = 10
GQ = 8


NORM_EPS = 1e-05
ROPE_BASE = 10000.0
BETA_ONE = 0.9
BETA_TWO = 0.95
ADAM_EPS = 1e-08
RATE = 0.1
GAIN_RATE = 1.0
DECAY = 0.1
NEGATIVE = -1e30


def from_behind(array, axis, by):
    count = lax.axis_size(axis)
    pairs = [(i, i + by) for i in range(count) if 0 <= i + by < count]
    return lax.ppermute(array, axis, pairs)


def rope_tables(first, count, seq_len):
    place = ((first + jnp.arange(count, dtype=jnp.int32)) % seq_len).astype(jnp.float32)
    freq = ROPE_BASE ** (-(jnp.arange(HD // 2, dtype=jnp.float32) * 2.0 / HD))
    angle = place[:, None] * freq[None, :]
    return (jnp.cos(angle)[:, None, :], jnp.sin(angle)[:, None, :])


def rotate(values, cosine, sine):
    half = values.shape[-1] // 2
    first, second = (values[..., :half], values[..., half:])
    return jnp.concatenate(
        [first * cosine - second * sine, second * cosine + first * sine], axis=-1
    )


def unrotate(grads, cosine, sine):
    half = grads.shape[-1] // 2
    first, second = (grads[..., :half], grads[..., half:])
    return jnp.concatenate(
        [first * cosine + second * sine, second * cosine - first * sine], axis=-1
    )


def token_total(values):
    return lax.psum(values, ("row", "col"))


def width_gather(values):
    return lax.all_gather(values, "col", axis=1, tiled=True)


def column_scatter(values):
    return lax.psum_scatter(values, "col", scatter_dimension=1, tiled=True)


def row_total(values):
    return lax.psum(values, "row")


def row_gather(values):
    return lax.all_gather(values, "row", axis=1, tiled=True)


def row_scatter(values):
    return lax.psum_scatter(values, "row", scatter_dimension=1, tiled=True)


def norm_scale(values):
    return lax.rsqrt(token_total(jnp.sum(values * values, axis=1)) / D + NORM_EPS)


def norm_back(upstream, values, scale, gain):
    weighted = upstream * gain[None, :]
    total = token_total(jnp.sum(weighted * values, axis=1))
    grad = scale[:, None] * weighted - values * (scale * scale * scale * total / D)[:, None]
    gain_grad = jnp.sum(upstream * values * scale[:, None], axis=0)
    return (grad, gain_grad)


def adam(weight, grad, first, second, rate, decay):
    first = BETA_ONE * first + (1.0 - BETA_ONE) * grad
    second = BETA_TWO * second + (1.0 - BETA_TWO) * grad * grad
    first_hat = first / (1.0 - BETA_ONE**STEP)
    second_hat = second / (1.0 - BETA_TWO**STEP)
    return (
        first,
        second,
        weight - rate * (first_hat / (jnp.sqrt(second_hat) + ADAM_EPS) + decay * weight),
    )


def body(
    inputs,
    segments,
    cotangent,
    w_qkv,
    w_out,
    w_gate_up,
    w_down,
    gains,
    first_qkv,
    second_qkv,
    first_out,
    second_out,
    first_gate_up,
    second_gate_up,
    first_down,
    second_down,
    first_gains,
    second_gains,
):
    low_type = jnp.bfloat16
    count = inputs.shape[0]
    data_count = lax.axis_size("dp")
    row_count = lax.axis_size("row")
    data_place = lax.axis_index("dp")
    row_place = lax.axis_index("row")
    seq_len = min(max(SEQ, 2 * count), count * data_count)
    group = seq_len // count
    my_heads = GQ // row_count
    lowered = (
        w_qkv.astype(low_type),
        w_out.astype(low_type),
        w_gate_up.astype(low_type),
        w_down.astype(low_type),
        gains.astype(low_type),
    )
    full_qkv, full_out, full_gate_up, full_down, full_gains = (
        lax.all_gather(lowered[0], "dp", axis=1, tiled=True),
        lax.all_gather(lowered[1], "dp", axis=1, tiled=True),
        lax.all_gather(lowered[2], "dp", axis=1, tiled=True),
        lax.all_gather(lowered[3], "dp", axis=1, tiled=True),
        lax.all_gather(lowered[4], "dp", axis=2, tiled=True),
    )
    weight_qkv = full_qkv[0, :, 0, :]
    weight_out = full_out[0]
    units = full_gate_up.shape[3]
    weight_gate_up = full_gate_up[0].reshape(full_gate_up.shape[1], 2 * units)
    weight_down = full_down[0]
    gain_one = full_gains[0, 0].astype(jnp.float32)
    gain_two = full_gains[1, 0].astype(jnp.float32)
    residual = inputs.astype(jnp.float32)
    scale_one = norm_scale(residual)
    normed_one = width_gather((residual * scale_one[:, None] * gain_one[None, :]).astype(low_type))
    mixed = row_total(jnp.dot(normed_one, weight_qkv, preferred_element_type=jnp.float32))
    cosine, sine = rope_tables(data_place * count, count, seq_len)
    query_start = row_place * (my_heads * HD)
    queries = lax.dynamic_slice_in_dim(mixed, query_start, my_heads * HD, 1).reshape(
        count, my_heads, HD
    )
    queries = rotate(queries, cosine, sine).astype(low_type)
    keys = rotate(mixed[:, GQ * HD : GQ * HD + HD][:, None, :], cosine, sine)[:, 0].astype(low_type)
    values = mixed[:, GQ * HD + HD :].astype(low_type)
    query_index = data_place * count + jnp.arange(count, dtype=jnp.int32)
    query_segment = lax.dynamic_slice_in_dim(segments, data_place * count, count)
    blocks = [jnp.concatenate([keys, values], axis=1)]
    sources = [data_place]
    for step in range(1, group):
        blocks.append(from_behind(blocks[-1], "dp", 1))
        sources.append((data_place - step) % data_count)
    masks = []
    live = []
    for source in sources:
        key_index = source * count + jnp.arange(count, dtype=jnp.int32)
        key_segment = lax.dynamic_slice_in_dim(segments, source * count, count)
        masks.append(
            (query_segment[:, None] == key_segment[None, :])
            & (query_index[:, None] >= key_index[None, :])
        )
        live.append((key_segment[count - 1] >= query_segment[0]) & (source <= data_place))

    def scores_of(index):
        return (
            jnp.einsum(
                "thd,sd->hts", queries, blocks[index][:, :HD], preferred_element_type=jnp.float32
            )
            * 0.125
        )

    stats = (
        jnp.full((my_heads, count), NEGATIVE, jnp.float32),
        jnp.zeros((my_heads, count), jnp.float32),
    )
    for index in range(group):
        stats_top, stats_total = stats
        stats_masked = jnp.where(masks[index][None], scores_of(index), NEGATIVE)
        new_top = jnp.maximum(stats_top, jnp.max(stats_masked, axis=2))
        expo = jnp.where(masks[index][None], jnp.exp(stats_masked - new_top[:, :, None]), 0.0)
        stats = (new_top, stats_total * jnp.exp(stats_top - new_top) + jnp.sum(expo, axis=2))
    top, total = stats

    def probs_of(index):
        masked = jnp.where(masks[index][None], scores_of(index), NEGATIVE)
        return jnp.where(
            masks[index][None], jnp.exp(masked - top[:, :, None]) / total[:, :, None], 0.0
        )

    attended = jnp.zeros((count, my_heads, HD), jnp.float32)
    for index in range(group):
        attended = attended + jnp.einsum(
            "hts,sd->thd",
            probs_of(index).astype(low_type),
            blocks[index][:, HD:],
            preferred_element_type=jnp.float32,
        )
    heads_all = row_gather(attended.reshape(count, my_heads * HD).astype(low_type))
    middle = residual + column_scatter(
        jnp.dot(heads_all, weight_out, preferred_element_type=jnp.float32)
    )
    scale_two = norm_scale(middle)
    normed_two = width_gather((middle * scale_two[:, None] * gain_two[None, :]).astype(low_type))
    gate_up_part = jnp.dot(normed_two, weight_gate_up, preferred_element_type=jnp.float32).reshape(
        count, 2, units
    )
    gate_up = lax.psum_scatter(gate_up_part, "row", scatter_dimension=2, tiled=True)
    gate = gate_up[:, 0]
    up_value = gate_up[:, 1]
    sigma = jax.nn.sigmoid(gate)
    swish = gate * sigma
    hidden = row_gather((swish * up_value).astype(low_type))
    layer_output = (
        middle + column_scatter(jnp.dot(hidden, weight_down, preferred_element_type=jnp.float32))
    ).astype(low_type)
    down_in = width_gather(cotangent)
    grad_down = jnp.dot(hidden.T, down_in, preferred_element_type=jnp.float32)
    hidden_grad = row_scatter(jnp.dot(down_in, weight_down.T, preferred_element_type=jnp.float32))
    gate_grad = hidden_grad * up_value * sigma * (1.0 + gate * (1.0 - sigma))
    up_grad = hidden_grad * swish
    unit_grads = lax.all_gather(
        jnp.stack([gate_grad, up_grad], axis=1).astype(low_type), "row", axis=2, tiled=True
    )
    unit_grads = unit_grads.reshape(count, 2 * units)
    grad_gate_up = jnp.dot(normed_two.T, unit_grads, preferred_element_type=jnp.float32)
    normed_two_grad = column_scatter(
        jnp.dot(unit_grads, weight_gate_up.T, preferred_element_type=jnp.float32)
    )
    middle_grad, gain_two_grad = norm_back(normed_two_grad, middle, scale_two, gain_two)
    middle_grad = cotangent.astype(jnp.float32) + middle_grad
    down_term = grad_down.reshape(1, grad_down.shape[0], grad_down.shape[1])
    gate_up_term = grad_gate_up.reshape(1, grad_gate_up.shape[0], 2, units)
    branch_in = width_gather(middle_grad.astype(low_type))
    grad_out = jnp.dot(heads_all.T, branch_in, preferred_element_type=jnp.float32)
    heads_grad = row_scatter(jnp.dot(branch_in, weight_out.T, preferred_element_type=jnp.float32))
    heads_grad = heads_grad.astype(low_type).reshape(count, my_heads, HD)
    delta = jnp.sum(heads_grad.astype(jnp.float32) * attended, axis=2).T
    query_grad = jnp.zeros((count, my_heads, HD), jnp.float32)
    empty_part = jnp.zeros((count, 2 * HD), jnp.float32)
    pair_grad = empty_part
    for index in range(group):
        grad_query_grad = query_grad
        block = blocks[index]
        probs = probs_of(index)
        inner = jnp.einsum(
            "thd,sd->hts", heads_grad, block[:, HD:], preferred_element_type=jnp.float32
        )
        score_grad = (probs * (inner - delta[:, :, None])).astype(low_type)
        grad_query_grad = (
            grad_query_grad
            + jnp.einsum(
                "hts,sd->thd", score_grad, block[:, :HD], preferred_element_type=jnp.float32
            )
            * 0.125
        )
        grad_key_grad = (
            jnp.einsum("hts,thd->sd", score_grad, queries, preferred_element_type=jnp.float32)
            * 0.125
        )
        grad_value_grad = jnp.einsum(
            "hts,thd->sd", probs.astype(low_type), heads_grad, preferred_element_type=jnp.float32
        )
        query_grad = grad_query_grad
        part = jnp.concatenate([grad_key_grad, grad_value_grad], axis=1)
        if index == 0:
            pair_grad = part
        else:
            pair_grad = pair_grad + from_behind(part, "dp", -index)
    query_grad = unrotate(query_grad, cosine, sine).reshape(count, my_heads * HD)
    key_grad = unrotate(pair_grad[:, :HD][:, None, :], cosine, sine)[:, 0]
    value_grad = pair_grad[:, HD:]
    query_block = lax.dynamic_update_slice_in_dim(
        jnp.zeros((count, GQ * HD), jnp.float32), query_grad, query_start, 1
    )
    mixed_grad = row_total(jnp.concatenate([query_block, key_grad, value_grad], axis=1)).astype(
        low_type
    )
    grad_qkv = jnp.dot(normed_one.T, mixed_grad, preferred_element_type=jnp.float32)
    normed_one_grad = column_scatter(
        jnp.dot(mixed_grad, weight_qkv.T, preferred_element_type=jnp.float32)
    )
    input_grad, gain_one_grad = norm_back(normed_one_grad, residual, scale_one, gain_one)
    input_grad = middle_grad + input_grad
    qkv_term = grad_qkv.reshape(1, grad_qkv.shape[0], 1, grad_qkv.shape[1])
    out_term = grad_out.reshape(1, grad_out.shape[0], grad_out.shape[1])
    gain_term = jnp.stack([gain_one_grad, gain_two_grad], axis=0)[:, None, :]
    qkv_sum, out_sum, gate_up_sum, down_sum, gain_sum = (
        lax.psum_scatter(qkv_term, "dp", scatter_dimension=1, tiled=True),
        lax.psum_scatter(out_term, "dp", scatter_dimension=1, tiled=True),
        lax.psum_scatter(gate_up_term, "dp", scatter_dimension=1, tiled=True),
        lax.psum_scatter(down_term, "dp", scatter_dimension=1, tiled=True),
        lax.psum_scatter(gain_term, "dp", scatter_dimension=2, tiled=True),
    )
    first_a, second_a, new_a = adam(w_qkv, qkv_sum, first_qkv, second_qkv, RATE, DECAY)
    first_b, second_b, new_b = adam(w_out, out_sum, first_out, second_out, RATE, DECAY)
    first_c, second_c, new_c = adam(
        w_gate_up, gate_up_sum, first_gate_up, second_gate_up, RATE, DECAY
    )
    first_d, second_d, new_d = adam(w_down, down_sum, first_down, second_down, RATE, DECAY)
    first_e, second_e, new_e = adam(gains, gain_sum, first_gains, second_gains, GAIN_RATE, 0.0)
    return (
        layer_output,
        input_grad,
        qkv_sum,
        first_a,
        second_a,
        new_a,
        out_sum,
        first_b,
        second_b,
        new_b,
        gate_up_sum,
        first_c,
        second_c,
        new_c,
        down_sum,
        first_d,
        second_d,
        new_d,
        gain_sum,
        first_e,
        second_e,
        new_e,
    )


def solution(mesh):
    placed = (
        P("dp", ("row", "col")),
        P(),
        P("dp", ("row", "col")),
        P("row", "dp", "col", None),
        P("col", "dp", "row"),
        P("row", "dp", None, "col"),
        P("col", "dp", "row"),
        P(None, ("row", "col"), "dp"),
        P("row", "dp", "col", None),
        P("row", "dp", "col", None),
        P("col", "dp", "row"),
        P("col", "dp", "row"),
        P("row", "dp", None, "col"),
        P("row", "dp", None, "col"),
        P("col", "dp", "row"),
        P("col", "dp", "row"),
        P(None, ("row", "col"), "dp"),
        P(None, ("row", "col"), "dp"),
    )
    return jax.shard_map(
        body,
        mesh=mesh,
        in_specs=placed,
        out_specs=(
            P("dp", ("row", "col")),
            P("dp", ("row", "col")),
            P("row", "dp", "col", None),
            P("row", "dp", "col", None),
            P("row", "dp", "col", None),
            P("row", "dp", "col", None),
            P("col", "dp", "row"),
            P("col", "dp", "row"),
            P("col", "dp", "row"),
            P("col", "dp", "row"),
            P("row", "dp", None, "col"),
            P("row", "dp", None, "col"),
            P("row", "dp", None, "col"),
            P("row", "dp", None, "col"),
            P("col", "dp", "row"),
            P("col", "dp", "row"),
            P("col", "dp", "row"),
            P("col", "dp", "row"),
            P(None, ("row", "col"), "dp"),
            P(None, ("row", "col"), "dp"),
            P(None, ("row", "col"), "dp"),
            P(None, ("row", "col"), "dp"),
        ),
        check_vma=False,
    )
```

profile of v0, /device:TPU:0, one launch (start us, length us, event | category | flops | bytes accessed | tf_op | source)
XLA Modules:
  0.0 1188.5 jit_solution(13030725011043260252)
XLA Ops:
  8.0 15.1 %all_gather.36 = bf16[2,1,256]{1,0,2:T(2,128)(2,1)S(1)} all-gather(bf16[2,1,64]{1,0,2:T(2,128)(2,1)S(1)} %copy.294), channel_id=1, replica_groups=mesh['dp'=4,'row'=2,'col'=4] {'dp'}, dimensions={2}, use_global_device_ids=true | all-gather | bytes 1280 | tf_op jit(solution)/shard_map/all_gather | solution.py:142
  25.9 14.3 %psum.42 = f32[512]{0:T(512)S(1)} all-reduce(f32[512]{0:T(512)S(1)} %fusion.53), channel_id=1, replica_groups=mesh['dp'=4,'row'=2,'col'=4] {'row','col'}, use_global_device_ids=true, to_apply=%region_1.0 | all-reduce | flops 512 | bytes 4096 | tf_op jit(solution)/shard_map/psum | solution.py:54
  44.0 25.8 %all-gather.11.cloned.1.call-done = bf16[512,1024]{1,0:T(8,128)(2,1)} async-done(((bf16[512,256]{1,0:T(8,128)(2,1)}), bf16[512,1024]{1,0:T(8,128)(2,1)}) %all-gather.11.cloned.1.call-update) | async-done | bytes 1048592 | tf_op jit(solution)/shard_map/all_gather | solution.py:58
  69.9 34.9 %all-gather.13.cloned.1.call-done = bf16[1,1024,1,640]{3,1,2,0:T(8,128)(2,1)} async-done(((bf16[1,256,1,640]{3,1,2,0:T(8,128)(2,1)}), bf16[1,1024,1,640]{3,1,2,0:T(8,128)(2,1)}) %all-gather.13.cloned.1.call-update) | async-done | bytes 1310736 | tf_op jit(solution)/shard_map/all_gather | solution.py:138
  111.1 16.4 %all-reduce.3.cloned.1.call-done = f32[512,640]{0,1:T(8,128)} async-done(((f32[512,640]{0,1:T(8,128)}), f32[512,640]{0,1:T(8,128)}) %all-reduce.3.cloned.1.call-update) | async-done | bytes 1310736 | tf_op jit(solution)/shard_map/psum | solution.py:66
  147.1 6.2 collective-permute-start.2
  181.9 35.1 %reduce-scatter.15.cloned.1.call-done = f32[512,256]{1,0:T(8,128)} async-done(((f32[512,1024]{1,0:T(8,128)}), f32[512,256]{1,0:T(8,128)}) %reduce-scatter.15.cloned.1.call-update) | async-done | bytes 524304 | tf_op jit(solution)/shard_map/reduce_scatter | solution.py:62
  218.3 14.9 %psum.44 = f32[512]{0:T(512)} all-reduce(f32[512]{0:T(512)S(1)} %get-tuple-element.153), channel_id=1, replica_groups=mesh['dp'=4,'row'=2,'col'=4] {'row','col'}, use_global_device_ids=true, to_apply=%region_13.14 | all-reduce | flops 512 | bytes 4096 | tf_op jit(solution)/shard_map/psum | solution.py:54
  235.7 9.6 all-gather.25.cloned.1.call-done
  245.3 61.4 %all-gather.23.cloned.1.call-done = bf16[1,1408,1024]{2,1,0:T(8,128)(2,1)} async-done(((bf16[1,352,1024]{2,1,0:T(8,128)(2,1)}), bf16[1,1408,1024]{2,1,0:T(8,128)(2,1)}) %all-gather.23.cloned.1.call-update) | async-done | bytes 2883600 | tf_op jit(solution)/shard_map/all_gather | solution.py:141
  312.1 102.1 %all-gather.19.cloned.1.call-done = bf16[1,1024,2,1408]{3,2,0,1:T(2,128)(2,1)} async-done(((bf16[1,256,2,1408]{3,2,0,1:T(2,128)(2,1)}), bf16[1,1024,2,1408]{3,2,0,1:T(2,128)(2,1)}) %all-gather.19.cloned.1.call-update) | async-done | bytes 5767184 | tf_op jit(solution)/shard_map/all_gather | solution.py:140
  420.3 8.3 copy.302
  428.7 12.7 %all-gather.17.cloned.1.call-done = bf16[512,1024]{1,0:T(8,128)(2,1)} async-done(((bf16[512,256]{1,0:T(8,128)(2,1)}), bf16[512,1024]{1,0:T(8,128)(2,1)}) %all-gather.17.cloned.1.call-update) | async-done | bytes 1048592 | tf_op jit(solution)/shard_map/all_gather | solution.py:58
  441.4 8.7 fusion.33
  454.6 17.5 %reduce-scatter.17.cloned.1.call-done = f32[512,2,704]{0,2,1:T(8,128)} async-done(((f32[512,2,1408]{0,2,1:T(8,128)}), f32[512,2,704]{0,2,1:T(8,128)}) %reduce-scatter.17.cloned.1.call-update) | async-done | bytes 2883600 | tf_op jit(solution)/shard_map/reduce_scatter | solution.py:224
  477.4 13.1 %all-gather.27.cloned.1.call-done = bf16[512,2,1408]{0,2,1:T(8,128)(2,1)} async-done(((bf16[512,2,704]{0,2,1:T(8,128)(2,1)}), bf16[512,2,1408]{0,2,1:T(8,128)(2,1)}) %all-gather.27.cloned.1.call-update) | async-done | bytes 2883600 | tf_op jit(solution)/shard_map/all_gather | solution.py:238
  490.5 8.0 fusion.115
  498.6 36.5 %reduce-scatter.23.cloned.1.call-done = f32[512,256]{1,0:T(8,128)} async-done(((f32[512,1024]{1,0:T(8,128)}), f32[512,256]{1,0:T(8,128)}) %reduce-scatter.23.cloned.1.call-update) | async-done | bytes 524304 | tf_op jit(solution)/shard_map/reduce_scatter | solution.py:62
  536.9 14.9 %psum.45 = f32[512]{0:T(512)} all-reduce(f32[512]{0:T(512)} %get-tuple-element.133), channel_id=1, replica_groups=mesh['dp'=4,'row'=2,'col'=4] {'row','col'}, use_global_device_ids=true, to_apply=%region_19.20 | all-reduce | flops 512 | bytes 4096 | tf_op jit(solution)/shard_map/psum | solution.py:54
  555.2 27.4 %all-gather.29.cloned.1.call-done = bf16[512,1024]{1,0:T(8,128)(2,1)} async-done(((bf16[512,256]{1,0:T(8,128)(2,1)}), bf16[512,1024]{1,0:T(8,128)(2,1)}) %all-gather.29.cloned.1.call-update) | async-done | bytes 1048592 | tf_op jit(solution)/shard_map/all_gather | solution.py:58
  586.9 7.7 reduce-scatter.25.cloned.1.call-done
  632.7 18.0 %collective-permute-done.4 = f32[512,128]{0,1:T(8,128)S(1)} collective-permute-done((f32[512,128]{0,1:T(8,128)S(1)}, f32[512,128]{0,1:T(8,128)S(1)}, u32[]{:S(2)}, u32[]{:S(2)}) %collective-permute-start.4) | collective-permute-done | bytes 262176 | tf_op jit(solution)/shard_map/ppermute | solution.py:27
  652.4 7.9 all-reduce.4
  679.6 18.2 %reduce-scatter.27.cloned.1.call-done = f32[512,256]{1,0:T(8,128)} async-done(((f32[512,1024]{1,0:T(8,128)}), f32[512,256]{1,0:T(8,128)}) %reduce-scatter.27.cloned.1.call-update) | async-done | bytes 524304 | tf_op jit(solution)/shard_map/reduce_scatter | solution.py:62
  706.2 10.0 convolution_bitcast_fusion
  716.2 28.8 %reduce-scatter.31.cloned.1.call-done = f32[1,128,1024]{2,1,0:T(8,128)} async-done(((f32[1,512,1024]{2,1,0:T(8,128)}), f32[1,128,1024]{2,1,0:T(8,128)}) %reduce-scatter.31.cloned.1.call-update) | async-done | bytes 524304 | tf_op jit(solution)/shard_map/reduce_scatter | solution.py:306
  748.0 101.5 %reduce-scatter.35.cloned.1.call-done = f32[1,352,1024]{2,1,0:T(8,128)} async-done(((f32[1,1408,1024]{2,1,0:T(8,128)}), f32[1,352,1024]{2,1,0:T(8,128)}) %reduce-scatter.35.cloned.1.call-update) | async-done | bytes 1441808 | tf_op jit(solution)/shard_map/reduce_scatter | solution.py:308
  855.2 14.7 %psum.47 = f32[512]{0:T(512)S(1)} all-reduce(f32[512]{0:T(512)S(1)} %get-tuple-element.135), channel_id=1, replica_groups=mesh['dp'=4,'row'=2,'col'=4] {'row','col'}, use_global_device_ids=true, to_apply=%region_25.26 | all-reduce | flops 512 | bytes 4096 | tf_op jit(solution)/shard_map/psum | solution.py:54
  869.9 19.2 %reduce-scatter.19.cloned.1.call-done = f32[512,256]{1,0:T(8,128)} async-done(((f32[512,1024]{1,0:T(8,128)}), f32[512,256]{1,0:T(8,128)}) %reduce-scatter.19.cloned.1.call-update) | async-done | bytes 524304 | tf_op jit(solution)/shard_map/reduce_scatter | solution.py:62
  891.7 19.4 %reduce-scatter.37.cloned.1.call-done = f32[64,2]{1,0:T(8,128)} async-done(((f32[256,2]{1,0:T(8,128)}), f32[64,2]{1,0:T(8,128)}) %reduce-scatter.37.cloned.1.call-update) | async-done | bytes 528
  912.7 51.6 %reduce-scatter.29.cloned.1.call-done = f32[1,256,1,640]{3,1,2,0:T(8,128)} async-done(((f32[1,1024,1,640]{3,1,2,0:T(8,128)}), f32[1,256,1,640]{3,1,2,0:T(8,128)}) %reduce-scatter.29.cloned.1.call-update) | async-done | bytes 655376 | tf_op jit(solution)/shard_map/reduce_scatter | solution.py:305
  972.7 188.7 %reduce-scatter.33.cloned.1.call-done = f32[1,256,2,1408]{3,1,2,0:T(8,128)} async-done(((f32[1,1024,2,1408]{3,1,2,0:T(8,128)}), f32[1,256,2,1408]{3,1,2,0:T(8,128)}) %reduce-scatter.33.cloned.1.call-update) | async-done | bytes 2883600 | tf_op jit(solution)/shard_map/reduce_scatter | solution.py:307
  (285 shorter events, 204.5 us)
Async XLA Ops:
  7.2 62.7 %all-gather.11.cloned.1.call-start = ((), (), s32[]{:S(2)}) async-start(), calls=%async_computation.12 | async-start | bytes 1310720 | tf_op jit(solution)/shard_map/all_gather | solution.py:58
  42.0 62.7 %all-gather.13.cloned.1.call-start = ((), (), s32[]{:S(2)}) async-start(), calls=%async_computation.13 | async-start | bytes 1638400 | tf_op jit(solution)/shard_map/all_gather | solution.py:138
  44.0 83.5 %all-reduce.3.cloned.1.call-start = ((), (), s32[]{:S(2)}) async-start(), calls=%async_computation.14 | async-start | bytes 2621440 | tf_op jit(solution)/shard_map/psum | solution.py:66
  108.4 64.8 %all-gather.15.cloned.1.call-start = ((), (), s32[]{:S(2)}) async-start(), calls=%async_computation.15 | async-start | bytes 1310720 | tf_op jit(solution)/shard_map/all_gather | solution.py:139
  109.2 107.8 %reduce-scatter.15.cloned.1.call-start = ((), (), s32[]{:S(2)}) async-start(), calls=%async_computation.16 | async-start | bytes 2621440 | tf_op jit(solution)/shard_map/reduce_scatter | solution.py:62
  129.7 6.9 collective-permute-start
  136.6 10.5 collective-permute-start.1
  147.1 11.4 collective-permute-start.2
  176.7 68.5 %all-gather.25.cloned.1.call-start = ((), (), s32[]{:S(2)}) async-start(), calls=%async_computation.23 | async-start | bytes 1310720 | tf_op jit(solution)/shard_map/all_gather | solution.py:58
  177.3 129.3 %all-gather.23.cloned.1.call-start = ((), (), s32[]{:S(2)}) async-start(), calls=%async_computation.21 | async-start | bytes 3604480 | tf_op jit(solution)/shard_map/all_gather | solution.py:141
  179.7 234.5 %all-gather.19.cloned.1.call-start = ((), (), s32[]{:S(2)}) async-start(), calls=%async_computation.18 | async-start | bytes 7208960 | tf_op jit(solution)/shard_map/all_gather | solution.py:140
  181.9 259.5 %all-gather.17.cloned.1.call-start = ((), (), s32[]{:S(2)}) async-start(), calls=%async_computation.17 | async-start | bytes 1310720 | tf_op jit(solution)/shard_map/all_gather | solution.py:58
  235.4 219.2 %reduce-scatter.21.cloned.1.call-start = ((), (), s32[]{:S(2)}) async-start(), calls=%async_computation.24 | async-start | bytes 4325376 | tf_op jit(solution)/shard_map/reduce_scatter | solution.py:74
  312.0 160.0 %reduce-scatter.17.cloned.1.call-start = ((), (), s32[]{:S(2)}) async-start(), calls=%async_computation.19 | async-start | bytes 8650752 | tf_op jit(solution)/shard_map/reduce_scatter | solution.py:224
  450.1 40.4 %all-gather.27.cloned.1.call-start = ((), (), s32[]{:S(2)}) async-start(), calls=%async_computation.25 | async-start | bytes 4325376 | tf_op jit(solution)/shard_map/all_gather | solution.py:238
  477.3 57.7 %reduce-scatter.23.cloned.1.call-start = ((), (), s32[]{:S(2)}) async-start(), calls=%async_computation.26 | async-start | bytes 2621440 | tf_op jit(solution)/shard_map/reduce_scatter | solution.py:62
  498.5 84.1 %all-gather.29.cloned.1.call-start = ((), (), s32[]{:S(2)}) async-start(), calls=%async_computation.27 | async-start | bytes 1310720 | tf_op jit(solution)/shard_map/all_gather | solution.py:58
  555.2 39.5 %reduce-scatter.25.cloned.1.call-start = ((), (), s32[]{:S(2)}) async-start(), calls=%async_computation.28 | async-start | bytes 1572864 | tf_op jit(solution)/shard_map/reduce_scatter | solution.py:74
  585.9 81.8 %all-gather.21.cloned.1.call-start = ((), (), s32[]{:S(2)}) async-start(), calls=%async_computation.20 | async-start | bytes 2162688 | tf_op jit(solution)/shard_map/all_gather | solution.py:70
  586.5 111.2 %reduce-scatter.27.cloned.1.call-start = ((), (), s32[]{:S(2)}) async-start(), calls=%async_computation.29 | async-start | bytes 2621440 | tf_op jit(solution)/shard_map/reduce_scatter | solution.py:62
  622.3 10.4 collective-permute-start.3
  623.6 27.1 %collective-permute-start.4 = (f32[512,128]{0,1:T(8,128)S(1)}, f32[512,128]{0,1:T(8,128)S(1)}, u32[]{:S(2)}, u32[]{:S(2)}) collective-permute-start(f32[512,128]{0,1:T(8,128)S(1)} %pad_maximum_fusion.5), channel_id=1, source_target_pairs={{16,0},{24,8},{17,1},{25,9},{18,2},{26,10},{19,3},{27,11},{20,4},{... | collective-permute-start | bytes 786440 | tf_op jit(solution)/shard_map/ppermute | solution.py:27
  624.9 25.8 %collective-permute-start.5 = (f32[512,128]{0,1:T(8,128)S(1)}, f32[512,128]{0,1:T(8,128)S(1)}, u32[]{:S(2)}, u32[]{:S(2)}) collective-permute-start(f32[512,128]{0,1:T(8,128)S(1)} %pad_maximum_fusion.6), channel_id=1, source_target_pairs={{24,0},{25,1},{26,2},{27,3},{28,4},{29,5},{30,6},{31,7}} | collective-permute-start | bytes 786440 | tf_op jit(solution)/shard_map/ppermute | solution.py:27
  664.2 80.8 %reduce-scatter.31.cloned.1.call-start = ((), (), s32[]{:S(2)}) async-start(), calls=%async_computation.31 | async-start | bytes 2621440 | tf_op jit(solution)/shard_map/reduce_scatter | solution.py:306
  667.7 181.8 %reduce-scatter.35.cloned.1.call-start = ((), (), s32[]{:S(2)}) async-start(), calls=%async_computation.33 | async-start | bytes 7208960 | tf_op jit(solution)/shard_map/reduce_scatter | solution.py:308
  673.9 215.1 %reduce-scatter.19.cloned.1.call-start = ((), (), s32[]{:S(2)}) async-start(), calls=%async_computation.22 | async-start | bytes 2621440 | tf_op jit(solution)/shard_map/reduce_scatter | solution.py:62
  679.5 231.6 %reduce-scatter.37.cloned.1.call-start = ((), (), s32[]{:S(2)}) async-start(), calls=%async_computation.34 | async-start | bytes 163840
  702.0 262.4 %reduce-scatter.29.cloned.1.call-start = ((), (), s32[]{:S(2)}) async-start(), calls=%async_computation.30 | async-start | bytes 3276800 | tf_op jit(solution)/shard_map/reduce_scatter | solution.py:305
  706.0 455.4 %reduce-scatter.33.cloned.1.call-start = ((), (), s32[]{:S(2)}) async-start(), calls=%async_computation.32 | async-start | bytes 14417920 | tf_op jit(solution)/shard_map/reduce_scatter | solution.py:307
  748.0 164.1 %copy-start.55 = (f32[2,1,64]{2,1,0:T(1,128)S(1)}, f32[2,1,64]{2,1,0:T(1,128)}, u32[]{:S(2)}) copy-start(f32[2,1,64]{2,1,0:T(1,128)} %param.25) | copy-start | bytes 1540
  748.0 164.1 %copy-start.56 = (f32[2,1,64]{2,1,0:T(1,128)S(1)}, f32[2,1,64]{2,1,0:T(1,128)}, u32[]{:S(2)}) copy-start(f32[2,1,64]{2,1,0:T(1,128)} %param.35) | copy-start | bytes 1540
  748.0 164.1 %copy-start.57 = (f32[2,1,64]{2,1,0:T(1,128)S(1)}, f32[2,1,64]{2,1,0:T(1,128)}, u32[]{:S(2)}) copy-start(f32[2,1,64]{2,1,0:T(1,128)} %param.34) | copy-start | bytes 1540
  (55 other events, 1503.5 us)
Sparse Core Ops, SparseCore 0:
  42.2 27.6 all-gather.10
  72.0 32.6 all-gather.12
  108.5 18.9 all-reduce.2
  129.6 31.7 all-gather.14
  176.8 40.1 reduce-scatter.14
  218.7 26.5 all-gather.24
  247.4 59.1 all-gather.22
  308.8 105.3 all-gather.18
  416.6 24.7 all-gather.16
  444.1 10.4 reduce-scatter.20
  457.0 15.0 reduce-scatter.16
  477.5 12.9 all-gather.26
  498.6 36.3 reduce-scatter.22
  555.3 27.3 all-gather.28
  586.0 8.5 reduce-scatter.24
  596.6 10.7 all-gather.20
  664.3 33.3 reduce-scatter.26
  701.1 43.8 reduce-scatter.30
  747.9 101.5 reduce-scatter.34
  852.9 36.0 reduce-scatter.18
  892.0 19.1 reduce-scatter.36
  914.0 50.3 reduce-scatter.28
  966.7 194.5 reduce-scatter.32
where the time goes:
time: 1190 us
  waiting for transfers between devices  867 us (73%)
  matrix products  97.9 us (8%)
  blocking collectives  84 us (7%)
  other arithmetic  53.9 us (5%)
  local copies, waits for them, and re-layouts  49.8 us (4%)
  starting transfers between devices  19.9 us (2%)
  between operations  15.6 us (1%)
    reduce_scatter x1, waiting for transfers between devices, body(): lax.psum_scatter(gate_up_term, 'dp', scatter_dimension=1, tiled=True)  189 us
    reduce_scatter x4, waiting for transfers between devices, column_scatter(): return lax.psum_scatter(values, 'col', scatter_dimension=1, tiled=True)  109 us
    all_gather x1, waiting for transfers between devices, body(): lax.all_gather(lowered[2], 'dp', axis=1, tiled=True)  102 us
    reduce_scatter x1, waiting for transfers between devices, body(): lax.psum_scatter(down_term, 'dp', scatter_dimension=1, tiled=True)  102 us
    all_gather x4, waiting for transfers between devices, width_gather(): return lax.all_gather(values, 'col', axis=1, tiled=True)  75.6 us
    all_gather x1, waiting for transfers between devices, body(): lax.all_gather(lowered[3], 'dp', axis=1, tiled=True)  61.4 us
    psum x4, blocking collectives, token_total(): return lax.psum(values, ('row', 'col'))  58.8 us
    reduce_scatter x1, waiting for transfers between devices, body(): lax.psum_scatter(qkv_term, 'dp', scatter_dimension=1, tiled=True)  51.6 us
  transfers between devices with their start and end apart: 29, of which 26 were waited for; matrix products, arithmetic and copies ran while one was open for 12% of the time, Pallas kernels for 0%

commit v1 on v0

--- a/solution.py
+++ b/solution.py
@@ -341,6 +341,324 @@
     )
 
 
+def gather_joint(block):
+    places = lax.axis_size("dp"), lax.axis_size("col")
+    rows, columns = block.shape
+    parts = lax.all_gather(block, ("dp", "col"), axis=0, tiled=False)
+    parts = parts.reshape(places + (rows, columns)).transpose(0, 2, 1, 3)
+    return parts.reshape(places[0] * rows, places[1] * columns)
+
+
+def gather_steps(block):
+    return width_gather(lax.all_gather(block, "dp", axis=0, tiled=True))
+
+
+def scatter_joint(whole):
+    data, cols = lax.axis_size("dp"), lax.axis_size("col")
+    rows, columns = whole.shape[0] // data, whole.shape[1] // cols
+    parts = whole.reshape(data, rows, cols, columns).transpose(0, 2, 1, 3)
+    parts = parts.reshape(data * cols, rows, columns)
+    return lax.psum_scatter(parts, ("dp", "col"), scatter_dimension=0, tiled=False).astype(
+        jnp.float32
+    )
+
+
+def scatter_steps(whole):
+    part = column_scatter(whole)
+    return lax.psum_scatter(part, "dp", scatter_dimension=0, tiled=True).astype(jnp.float32)
+
+
+def swap(values):
+    return lax.ppermute(values, "row", [(0, 1), (1, 0)])
+
+
+def in_order(is_first, mine, theirs):
+    return jnp.concatenate(
+        [jnp.where(is_first, mine, theirs), jnp.where(is_first, theirs, mine)], axis=1
+    )
+
+
+def exchange(values):
+    return lax.all_to_all(values, "dp", split_axis=0, concat_axis=0, tiled=True)
+
+
+def dot(left, right):
+    return jnp.dot(left, right, preferred_element_type=jnp.float32)
+
+
+def dot_rows(left, right):
+    return lax.dot_general(left, right, (((0,), (0,)), ((), ())), preferred_element_type=jnp.float32)
+
+
+def dot_columns(left, right):
+    return lax.dot_general(left, right, (((1,), (1,)), ((), ())), preferred_element_type=jnp.float32)
+
+
+def attend(queries, keys, values, segments, block):
+    tokens = queries.shape[0]
+    index = jnp.arange(tokens, dtype=jnp.int32)
+    outs, kept = [], []
+    for start in range(0, tokens, block):
+        stop = start + block
+        mask = (segments[start:stop, None] == segments[None, :stop]) & (
+            index[start:stop, None] >= index[None, :stop]
+        )
+        scores = dot_columns(queries[start:stop], keys[:stop]) * 0.125
+        scores = jnp.where(mask, scores, NEGATIVE)
+        expo = jnp.exp(scores - jnp.max(scores, axis=1, keepdims=True))
+        expo = jnp.where(mask, expo, 0.0)
+        probs = expo / jnp.sum(expo, axis=1, keepdims=True)
+        outs.append(dot(probs.astype(jnp.bfloat16), values[:stop]))
+        kept.append(probs)
+    return jnp.concatenate(outs, axis=0), kept
+
+
+def attend_back(queries, keys, values, kept, attended, upstream, block):
+    tokens = queries.shape[0]
+    low_type = jnp.bfloat16
+    delta = jnp.sum(upstream.astype(jnp.float32) * attended, axis=1, keepdims=True)
+    query_grads = []
+    key_grads = [0.0] * (tokens // block)
+    value_grads = [0.0] * (tokens // block)
+    for place, start in enumerate(range(0, tokens, block)):
+        stop = start + block
+        probs = kept[place]
+        inner = dot_columns(upstream[start:stop], values[:stop])
+        score_grad = (probs * (inner - delta[start:stop])).astype(low_type)
+        query_grads.append(dot(score_grad, keys[:stop]) * 0.125)
+        key_part = dot_rows(score_grad, queries[start:stop]) * 0.125
+        value_part = dot_rows(probs.astype(low_type), upstream[start:stop])
+        for piece in range(place + 1):
+            rows = slice(piece * block, (piece + 1) * block)
+            key_grads[piece] = key_grads[piece] + key_part[rows]
+            value_grads[piece] = value_grads[piece] + value_part[rows]
+    return (
+        jnp.concatenate(query_grads, axis=0),
+        jnp.concatenate(key_grads, axis=0),
+        jnp.concatenate(value_grads, axis=0),
+    )
+
+
+def body_units(
+    inputs,
+    segments,
+    cotangent,
+    w_qkv,
+    w_out,
+    w_gate_up,
+    w_down,
+    gains,
+    first_qkv,
+    second_qkv,
+    first_out,
+    second_out,
+    first_gate_up,
+    second_gate_up,
+    first_down,
+    second_down,
+    first_gains,
+    second_gains,
+):
+    low_type = jnp.bfloat16
+    count, width = inputs.shape
+    data_count = lax.axis_size("dp")
+    col_count = lax.axis_size("col")
+    data_place = lax.axis_index("dp")
+    row_place = lax.axis_index("row")
+    col_place = lax.axis_index("col")
+    is_first = row_place == 0
+    tokens = count * data_count
+    half = width * col_count
+    my_rows = w_qkv.shape[1]
+    units = w_down.shape[1]
+    own = units // 2
+
+    whole_in = gather_joint(inputs)
+    low_qkv = w_qkv[0, :, 0, :].astype(low_type)
+    query_part = low_qkv[:, : GQ * HD].reshape(my_rows, data_count, 2 * HD).transpose(1, 0, 2)
+    pair_part = jnp.broadcast_to(low_qkv[None, :, GQ * HD :], (data_count, my_rows, 2 * HD))
+    weight_qkv = exchange(
+        jnp.concatenate([query_part, pair_part], axis=2).reshape(data_count * my_rows, 4 * HD)
+    )
+    low_gains = lax.all_gather(gains[:, 0, :].astype(low_type), ("col", "dp"), axis=1, tiled=True)
+    gain_one = low_gains[0].astype(jnp.float32)
+    gain_two = low_gains[1].astype(jnp.float32)
+    weight_gate_up = exchange(
+        w_gate_up[0]
+        .astype(low_type)
+        .reshape(my_rows, 2, data_count, 2, own)
+        .transpose(2, 0, 3, 1, 4)
+        .reshape(data_count * my_rows, 4 * own)
+    )
+    whole_cot = gather_steps(cotangent)
+    weight_out = w_out[0].astype(low_type)
+    weight_down = w_down[0].astype(low_type)
+
+    wide = whole_in.astype(jnp.float32)
+    scale_one = lax.rsqrt(row_total(jnp.sum(wide * wide, axis=1)) / D + NORM_EPS)
+    normed_one = (wide * scale_one[:, None] * gain_one[None, :]).astype(low_type)
+    mixed = dot(normed_one, weight_qkv)
+    mine = jnp.where(is_first, mixed[:, :HD], mixed[:, HD : 2 * HD])
+    theirs = jnp.where(is_first, mixed[:, HD : 2 * HD], mixed[:, :HD])
+    pair = mixed[:, 2 * HD :]
+    arrived = swap(jnp.concatenate([theirs, pair], axis=1).astype(low_type)).astype(jnp.float32)
+    mixed = jnp.concatenate([mine, pair], axis=1) + arrived
+    cosine, sine = rope_tables(0, tokens, tokens)
+    cosine, sine = cosine[:, 0], sine[:, 0]
+    queries = rotate(mixed[:, :HD], cosine, sine).astype(low_type)
+    keys = rotate(mixed[:, HD : 2 * HD], cosine, sine).astype(low_type)
+    values = mixed[:, 2 * HD :].astype(low_type)
+    attended, kept = attend(queries, keys, values, segments, count)
+    low_attended = attended.astype(low_type)
+    heads = in_order(is_first, low_attended, swap(low_attended))
+    middle = inputs.astype(jnp.float32) + scatter_joint(dot(heads, weight_out).astype(low_type))
+    whole_middle = gather_steps(middle.astype(low_type)).astype(jnp.float32)
+    scale_two = lax.rsqrt(
+        row_total(jnp.sum(whole_middle * whole_middle, axis=1)) / D + NORM_EPS
+    )
+    normed_two = (whole_middle * scale_two[:, None] * gain_two[None, :]).astype(low_type)
+
+    mine_place = row_place * (2 * own)
+    their_place = (1 - row_place) * (2 * own)
+    mine_weight = lax.dynamic_slice_in_dim(weight_gate_up, mine_place, 2 * own, 1)
+    their_weight = lax.dynamic_slice_in_dim(weight_gate_up, their_place, 2 * own, 1)
+    arrived = swap(dot(normed_two, their_weight).astype(low_type))
+    gate_up = dot(normed_two, mine_weight) + arrived.astype(jnp.float32)
+    gate, up_value = gate_up[:, :own], gate_up[:, own:]
+    sigma = jax.nn.sigmoid(gate)
+    swish = gate * sigma
+    low_hidden = (swish * up_value).astype(low_type)
+    hidden = in_order(is_first, low_hidden, swap(low_hidden))
+    down = scatter_joint(dot(hidden, weight_down).astype(low_type))
+    layer_output = (middle + down).astype(low_type)
+
+    mine_down = lax.dynamic_slice_in_dim(weight_down, row_place * own, own, 0)
+    their_down = lax.dynamic_slice_in_dim(weight_down, (1 - row_place) * own, own, 0)
+    arrived = swap(dot_columns(whole_cot, their_down).astype(low_type))
+    hidden_grad = dot_columns(whole_cot, mine_down) + arrived.astype(jnp.float32)
+    grad_down = dot_rows(hidden, whole_cot)
+    gate_grad = hidden_grad * up_value * sigma * (1.0 + gate * (1.0 - sigma))
+    up_grad = hidden_grad * swish
+    unit_grads = jnp.concatenate([gate_grad, up_grad], axis=1).astype(low_type)
+    unit_grads = in_order(is_first, unit_grads, swap(unit_grads))
+    normed_two_grad = scatter_steps(dot_columns(unit_grads, weight_gate_up).astype(low_type))
+    grad_gate_up = dot_rows(normed_two, unit_grads).astype(low_type)
+    whole_grad = gather_joint(normed_two_grad.astype(low_type)).astype(jnp.float32)
+    total_two = row_total(jnp.sum(whole_grad * gain_two[None, :] * whole_middle, axis=1))
+    shrink_two = scale_two * scale_two * scale_two * total_two / D
+    branch_in = (
+        whole_cot.astype(jnp.float32)
+        + scale_two[:, None] * (whole_grad * gain_two[None, :])
+        - whole_middle * shrink_two[:, None]
+    ).astype(low_type)
+    gain_two_grad = jnp.sum(whole_grad * whole_middle * scale_two[:, None], axis=0)
+
+    def my_tokens(stat):
+        return lax.dynamic_slice_in_dim(stat, data_place * count, count)
+
+    def my_width(gain):
+        return lax.dynamic_slice_in_dim(gain, col_place * width, width)
+
+    middle_grad = (
+        cotangent.astype(jnp.float32)
+        + my_tokens(scale_two)[:, None] * (normed_two_grad * my_width(gain_two)[None, :])
+        - middle * my_tokens(shrink_two)[:, None]
+    )
+    grad_out = dot_rows(heads, branch_in)
+    heads_grad = dot_columns(branch_in, weight_out)
+    mine = jnp.where(is_first, heads_grad[:, :HD], heads_grad[:, HD:])
+    theirs = jnp.where(is_first, heads_grad[:, HD:], heads_grad[:, :HD])
+    heads_grad = (mine + swap(theirs.astype(low_type)).astype(jnp.float32)).astype(low_type)
+    query_grad, key_grad, value_grad = attend_back(
+        queries, keys, values, kept, attended, heads_grad, count
+    )
+    query_grad = unrotate(query_grad, cosine, sine).astype(low_type)
+    pair_grad = jnp.concatenate([unrotate(key_grad, cosine, sine), value_grad], axis=1)
+    sent = jnp.concatenate([query_grad, pair_grad.astype(low_type)], axis=1)
+    arrived = swap(sent)
+    mixed_grad = jnp.concatenate(
+        [
+            in_order(is_first, query_grad, arrived[:, :HD]),
+            (pair_grad + arrived[:, HD:].astype(jnp.float32)).astype(low_type),
+        ],
+        axis=1,
+    )
+    part_one = dot_columns(mixed_grad, weight_qkv)
+    normed_one_grad = scatter_steps(part_one.astype(low_type))
+    grad_qkv = dot_rows(normed_one, mixed_grad).astype(low_type)
+    weighted = part_one * wide
+    token_part = jnp.sum(weighted * gain_one[None, :], axis=1)
+    gain_part = lax.dynamic_update_slice_in_dim(
+        jnp.zeros((2 * half,), jnp.float32),
+        jnp.sum(weighted * scale_one[:, None], axis=0),
+        row_place * half,
+        0,
+    )
+    totals = lax.psum(jnp.concatenate([token_part, gain_part]), ("dp", "row", "col"))
+    shrink_one = my_tokens(scale_one * scale_one * scale_one * totals[:tokens] / D)
+    input_grad = (
+        middle_grad
+        + my_tokens(scale_one)[:, None] * (normed_one_grad * my_width(gain_one)[None, :])
+        - inputs.astype(jnp.float32) * shrink_one[:, None]
+    )
+    share = width // data_count
+    gain_start = col_place * width + data_place * share
+    gain_sum = jnp.stack(
+        [
+            lax.dynamic_slice_in_dim(totals, tokens + row_place * half + gain_start, share),
+            lax.dynamic_slice_in_dim(gain_two_grad, gain_start, share),
+        ]
+    )[:, None, :]
+    gate_up_sum = (
+        exchange(grad_gate_up)
+        .reshape(data_count, my_rows, 2, 2, own)
+        .transpose(1, 3, 0, 2, 4)
+        .reshape(1, my_rows, 2, data_count * units)
+        .astype(jnp.float32)
+    )
+    qkv_parts = exchange(grad_qkv).reshape(data_count, my_rows, 4 * HD).astype(jnp.float32)
+    qkv_sum = jnp.concatenate(
+        [
+            qkv_parts[:, :, : 2 * HD].transpose(1, 0, 2).reshape(my_rows, GQ * HD),
+            jnp.sum(qkv_parts[:, :, 2 * HD :], axis=0),
+        ],
+        axis=1,
+    )[None, :, None, :]
+    out_sum = grad_out[None]
+    down_sum = grad_down[None]
+    first_a, second_a, new_a = adam(w_qkv, qkv_sum, first_qkv, second_qkv, RATE, DECAY)
+    first_b, second_b, new_b = adam(w_out, out_sum, first_out, second_out, RATE, DECAY)
+    first_c, second_c, new_c = adam(
+        w_gate_up, gate_up_sum, first_gate_up, second_gate_up, RATE, DECAY
+    )
+    first_d, second_d, new_d = adam(w_down, down_sum, first_down, second_down, RATE, DECAY)
+    first_e, second_e, new_e = adam(gains, gain_sum, first_gains, second_gains, GAIN_RATE, 0.0)
+    return (
+        layer_output,
+        input_grad,
+        qkv_sum,
+        first_a,
+        second_a,
+        new_a,
+        out_sum,
+        first_b,
+        second_b,
+        new_b,
+        gate_up_sum,
+        first_c,
+        second_c,
+        new_c,
+        down_sum,
+        first_d,
+        second_d,
+        new_d,
+        gain_sum,
+        first_e,
+        second_e,
+        new_e,
+    )
+
+
 def solution(mesh):
     placed = (
         P("dp", ("row", "col")),
@@ -362,8 +680,9 @@
         P(None, ("row", "col"), "dp"),
         P(None, ("row", "col"), "dp"),
     )
+    whole_heads = mesh.shape["dp"] * mesh.shape["row"] == GQ and mesh.shape["row"] == 2
     return jax.shard_map(
-        body,
+        body_units if whole_heads else body,
         mesh=mesh,
         in_specs=placed,
         out_specs=(

time: 1190 us -> 868 us (0.73)
  waiting for transfers between devices: 867 us -> 447 us
  local copies, waits for them, and re-layouts: 49.8 us -> 110 us
  other arithmetic: 53.9 us -> 81.1 us
  blocking collectives: 84 us -> 110 us
  matrix products: 97.9 us -> 77.4 us
    reduce_scatter x7 -> x4, waiting for transfers between devices: 400 us -> 141 us  [the longest x2 93.8 us: scatter_joint(): lax.psum_scatter(parts, ('dp', 'col'), scatter_dimension=0, tiled=False)]
    all_gather x6 -> x4, waiting for transfers between devices: 211 us -> 146 us  [the longest x2 89.8 us: gather_joint(): parts = lax.all_gather(block, ('dp', 'col'), axis=0, tiled=False)]
    reduce_scatter x4 -> x2, waiting for transfers between devices: 109 us -> 52.8 us  [column_scatter(): return lax.psum_scatter(values, 'col', scatter_dimension=1, tiled=True)]
    all_to_all x0 -> x4, waiting for transfers between devices: none -> 53.7 us  [exchange(): return lax.all_to_all(values, 'dp', split_axis=0, concat_axis=0, tiled=True)]
    all_gather x2 -> x1, blocking collectives: 17.2 us -> 57.2 us  [body_units(): lax.all_gather(gains[:, 0, :].astype(low_type), ('col', 'dp'), axis=1, ti...]
    all_gather x4 -> x2, waiting for transfers between devices: 75.6 us -> 42.3 us  [width_gather(): return lax.all_gather(values, 'col', axis=1, tiled=True)]
    ppermute x6 -> x8, waiting for transfers between devices: 34.1 us -> 9.56 us  [swap(): return lax.ppermute(values, 'row', [(0, 1), (1, 0)])]
    unnamed x130 -> x180, local copies, waits for them, and re-layouts: 36.4 us -> 59.4 us
  transfers between devices with their start and end apart: 29 -> 24, of which waited for: 26 -> 17; matrix products, arithmetic and copies ran while one was open for 12% -> 17% of each run, Pallas kernels for 0% -> 0%
where the time goes in v1:
time: 868 us; the launch traced here: 861 us
  waiting for transfers between devices  447 us (51%)
  local copies, waits for them, and re-layouts  110 us (13%)
  blocking collectives  110 us (13%)
  other arithmetic  81.1 us (9%)
  matrix products  77.4 us (9%)
  starting transfers between devices  20.3 us (2%)
  between operations  15.8 us (2%)
    reduce_scatter x2, waiting for transfers between devices, scatter_joint(): lax.psum_scatter(parts, ('dp', 'col'), scatter_dimension=0, tiled=False)  93.8 us
    all_gather x2, waiting for transfers between devices, gather_joint(): parts = lax.all_gather(block, ('dp', 'col'), axis=0, tiled=False)  89.8 us
    unnamed x180, local copies, waits for them, and re-layouts  59.4 us
    all_gather x1, blocking collectives, body_units(): lax.all_gather(gains[:, 0, :].astype(low_type), ('col', 'dp'), axis=1, ti...  57.2 us
    all_gather x2, waiting for transfers between devices, gather_steps(): return width_gather(lax.all_gather(block, 'dp', axis=0, tiled=True))  56.1 us
    all_to_all x4, waiting for transfers between devices, exchange(): return lax.all_to_all(values, 'dp', split_axis=0, concat_axis=0, tiled=True)  53.7 us
    reduce_scatter x2, waiting for transfers between devices, column_scatter(): return lax.psum_scatter(values, 'col', scatter_dimension=1, tiled=True)  52.8 us
    reduce_scatter x2, waiting for transfers between devices, scatter_steps(): lax.psum_scatter(part, 'dp', scatter_dimension=0, tiled=True)  47.2 us
  transfers between devices with their start and end apart: 24, of which 17 were waited for; matrix products, arithmetic and copies ran while one was open for 17% of the time, Pallas kernels for 0%

profile of v1, /device:TPU:0, one launch (start us, length us, event | category | flops | bytes accessed | tf_op | source)
XLA Modules:
  0.0 861.0 jit_solution(6509847371391837533)
XLA Ops:
  10.2 6.3 all-to-all-start
  16.6 57.2 %all-gather.1 = bf16[2,1,1024]{1,0,2:T(2,128)(2,1)S(1)} all-gather(bf16[2,1,64]{1,0,2:T(2,128)(2,1)S(1)} %copy.144), channel_id=3, replica_groups=mesh['dp'=4,'row'=2,'col'=4] {'col','dp'}, dimensions={2}, use_global_device_ids=true | all-gather | bytes 4352 | tf_op jit(solution)/shard_map/all_gather | solution.py:483
  74.6 5.6 fusion.169
  82.9 12.5 %all-gather.18.cloned.1.call-done = bf16[8192,256]{1,0:T(8,128)(2,1)} async-done(((bf16[512,256]{1,0:T(8,128)(2,1)}), bf16[8192,256]{1,0:T(8,128)(2,1)}) %all-gather.18.cloned.1.call-update) | async-done | bytes 4194320 | tf_op jit(solution)/shard_map/all_gather | solution.py:347
  104.2 7.8 fusion.179
  140.5 7.9 reshape.404
  153.3 93.8 %reduce-scatter.7.cloned.1.call-done = bf16[1,512,256]{2,1,0:T(8,128)(2,1)} async-done(((bf16[16,512,256]{2,1,0:T(8,128)(2,1)}), bf16[1,512,256]{2,1,0:T(8,128)(2,1)}) %reduce-scatter.7.cloned.1.call-update) | async-done | bytes 262160 | tf_op jit(solution)/shard_map/reduce_scatter | solution.py:361
  249.6 27.3 %all-gather.10.cloned.1.call-done = bf16[2048,256]{1,0:T(8,128)(2,1)} async-done(((bf16[512,256]{1,0:T(8,128)(2,1)}), bf16[2048,256]{1,0:T(8,128)(2,1)}) %all-gather.10.cloned.1.call-update) | async-done | bytes 1048592 | tf_op jit(solution)/shard_map/all_gather | solution.py:353
  276.9 28.8 %all-gather.14.cloned.1.call-done = bf16[2048,256]{1,0:T(8,128)(2,1)} async-done(((bf16[512,256]{1,0:T(8,128)(2,1)}), bf16[2048,256]{1,0:T(8,128)(2,1)}) %all-gather.14.cloned.1.call-update) | async-done | bytes 1048592 | tf_op jit(solution)/shard_map/all_gather | solution.py:353
  305.8 5.6 copy.148
  318.9 34.3 %all-to-all-done.1 = bf16[4,256,704]{1,2,0:T(8,128)(2,1)} async-done(((bf16[4,256,704]{1,2,0:T(8,128)(2,1)}), bf16[4,256,704]{1,2,0:T(8,128)(2,1)}, u32[]{:S(2)}, u32[]{:S(2)}) %all-to-all-start.1) | async-done | bytes 1441824 | tf_op jit(solution)/shard_map/all_to_all | solution.py:382
  366.8 5.8 convolution_convert_fusion.3
  375.2 38.6 %all-gather.16.cloned.1.call-done = bf16[2048,1024]{1,0:T(8,128)(2,1)} async-done(((bf16[2048,256]{1,0:T(8,128)(2,1)}), bf16[2048,1024]{1,0:T(8,128)(2,1)}) %all-gather.16.cloned.1.call-update) | async-done | bytes 4194320 | tf_op jit(solution)/shard_map/all_gather | solution.py:58
  438.5 52.8 %reduce-scatter.11.cloned.1.call-done = bf16[2048,256]{1,0:T(8,128)(2,1)} async-done(((bf16[2048,1024]{1,0:T(8,128)(2,1)}), bf16[2048,256]{1,0:T(8,128)(2,1)}) %reduce-scatter.11.cloned.1.call-update) | async-done | bytes 1048592 | tf_op jit(solution)/shard_map/reduce_scatter | solution.py:62
  491.4 29.5 %reduce-scatter.13.cloned.1.call-done = bf16[512,256]{1,0:T(8,128)(2,1)} async-done(((bf16[2048,256]{1,0:T(8,128)(2,1)}), bf16[512,256]{1,0:T(8,128)(2,1)}) %reduce-scatter.13.cloned.1.call-update) | async-done | bytes 262160 | tf_op jit(solution)/shard_map/reduce_scatter | solution.py:368
  521.1 77.3 %all-gather.20.cloned.1.call-done = bf16[8192,256]{1,0:T(8,128)(2,1)} async-done(((bf16[512,256]{1,0:T(8,128)(2,1)}), bf16[8192,256]{1,0:T(8,128)(2,1)}) %all-gather.20.cloned.1.call-update) | async-done | bytes 4194320 | tf_op jit(solution)/shard_map/all_gather | solution.py:347
  598.4 6.4 convert_bitcast_fusion
  604.8 12.1 %copy.152 = f32[4,512,4,256]{3,2,1,0:T(4,128)} copy(f32[4,512,4,256]{3,1,2,0:T(8,128)} %convert_bitcast_fusion) | data formatting | bytes 16777216 | tf_op jit(solution)/shard_map/convert_element_type | solution.py:546
  616.9 5.6 copy.174
  630.2 7.0 fusion.5
  669.6 8.0 reshape.406
  695.0 5.6 copy.160
  700.6 5.7 copy.159
  708.2 8.6 multiply_subtract_fusion.1
  716.8 19.4 %all-to-all-done.3 = bf16[4,256,704]{1,2,0:T(8,128)(2,1)S(1)} async-done(((bf16[4,256,704]{1,2,0:T(8,128)(2,1)}), bf16[4,256,704]{1,2,0:T(8,128)(2,1)S(1)}, u32[]{:S(2)}, u32[]{:S(2)}) %all-to-all-start.3) | async-done | bytes 1441824 | tf_op jit(solution)/shard_map/all_to_all | solution.py:382
  738.3 5.7 copy.163
  744.0 6.4 multiply_subtract_fusion
  756.0 5.7 copy.165
  771.0 6.0 fusion.30
  781.5 42.9 %psum.31 = f32[4096]{0:T(1024)S(1)} all-reduce(f32[4096]{0:T(1024)S(1)} %pad_maximum_fusion.29), channel_id=1, replica_groups=mesh['dp'=4,'row'=2,'col'=4] {'dp','row','col'}, use_global_device_ids=true, to_apply=%region_23.24 | all-reduce | flops 4096 | bytes 32768 | tf_op jit(solution)/shard_map/psum | solution.py:597
  827.8 6.1 multiply_subtract_fusion.2
  833.9 17.7 %reduce-scatter.17.cloned.1.call-done = bf16[512,256]{1,0:T(8,128)(2,1)} async-done(((bf16[2048,256]{1,0:T(8,128)(2,1)}), bf16[512,256]{1,0:T(8,128)(2,1)}) %reduce-scatter.17.cloned.1.call-update) | async-done | bytes 262160 | tf_op jit(solution)/shard_map/reduce_scatter | solution.py:368
  (350 shorter events, 185.1 us)
Async XLA Ops:
  7.2 88.1 %all-gather.18.cloned.1.call-start = ((), (), s32[]{:S(2)}) async-start(), calls=%async_computation.20 | async-start | bytes 4456448 | tf_op jit(solution)/shard_map/all_gather | solution.py:347
  7.9 72.3 %copy-start.62 = (s32[2048]{0:T(1024)S(1)}, s32[2048]{0:T(1024)}, u32[]{:S(2)}) copy-start(s32[2048]{0:T(1024)} %param.19) | copy-start | bytes 24580
  10.2 72.5 %all-to-all-start = ((bf16[4,256,256]{1,2,0:T(8,128)(2,1)}), bf16[4,256,256]{1,2,0:T(8,128)(2,1)S(1)}, u32[]{:S(2)}, u32[]{:S(2)}) async-start(bf16[4,256,256]{1,2,0:T(8,128)(2,1)} %pad_maximum_fusion.14), calls=%async_computation | async-start | bytes 1048576 | tf_op jit(solution)/shard_map/all_to_all | solution.py:382
  16.5 230.7 %reduce-scatter.7.cloned.1.call-start = ((), (), s32[]{:S(2)}) async-start(), calls=%async_computation.10 | async-start | bytes 4456448 | tf_op jit(solution)/shard_map/reduce_scatter | solution.py:361
  80.9 44.0 %copy-start.72 = (s32[512]{0:T(512)}, s32[512]{0:T(512)S(1)}, u32[]{:S(2)}) copy-start(s32[512]{0:T(512)S(1)} %iota_add_fusion.3) | copy-start | bytes 6148
  82.6 42.2 %copy-start.63 = (s32[1536]{0:T(1024)}, s32[1536]{0:T(1024)S(1)}, u32[]{:S(2)}) copy-start(s32[1536]{0:T(1024)S(1)} %iota_add_fusion) | copy-start | bytes 18436
  82.9 30.3 %copy-start.50 = (bf16[4,256,256]{2,1,0:T(8,128)(2,1)}, bf16[4,256,256]{2,1,0:T(8,128)(2,1)S(1)}, u32[]{:S(2)}) copy-start(bf16[4,256,256]{2,1,0:T(8,128)(2,1)S(1)} %copy.146) | copy-start | bytes 1572868
  114.7 2.4 collective-permute-start
  134.8 1.6 collective-permute-start.1
  153.3 123.6 %all-gather.10.cloned.1.call-start = ((), (), s32[]{:S(2)}) async-start(), calls=%async_computation.11 | async-start | bytes 1310720 | tf_op jit(solution)/shard_map/all_gather | solution.py:353
  249.0 56.8 %all-gather.14.cloned.1.call-start = ((), (), s32[]{:S(2)}) async-start(), calls=%async_computation.14 | async-start | bytes 1310720 | tf_op jit(solution)/shard_map/all_gather | solution.py:353
  249.5 110.0 %all-gather.12.cloned.1.call-start = ((), (), s32[]{:S(2)}) async-start(), calls=%async_computation.12 | async-start | bytes 5242880 | tf_op jit(solution)/shard_map/all_gather | solution.py:58
  276.9 136.9 %all-gather.16.cloned.1.call-start = ((), (), s32[]{:S(2)}) async-start(), calls=%async_computation.15 | async-start | bytes 5242880 | tf_op jit(solution)/shard_map/all_gather | solution.py:58
  314.5 38.7 %all-to-all-start.1 = ((bf16[4,256,704]{1,2,0:T(8,128)(2,1)}), bf16[4,256,704]{1,2,0:T(8,128)(2,1)}, u32[]{:S(2)}, u32[]{:S(2)}) async-start(bf16[4,256,704]{1,2,0:T(8,128)(2,1)} %bitcast.153), calls=%async_computation.2 | async-start | bytes 2883584 | tf_op jit(solution)/shard_map/all_to_all | solution.py:382
  318.9 172.5 %reduce-scatter.11.cloned.1.call-start = ((), (), s32[]{:S(2)}) async-start(), calls=%async_computation.16 | async-start | bytes 5242880 | tf_op jit(solution)/shard_map/reduce_scatter | solution.py:62
  372.7 45.8 %collective-permute-start.2 = (bf16[2048,352]{0,1:T(8,128)(2,1)}, bf16[2048,352]{0,1:T(8,128)(2,1)}, u32[]{:S(2)}, u32[]{:S(2)}) collective-permute-start(bf16[2048,352]{0,1:T(8,128)(2,1)} %convolution_convert_fusion.3), channel_id=1, source_target_pairs={{0,4},{4,0},{1,5},{5,1},{2,6},{6,2},{3,7},{7,3},{8,12},{12,8},{9,1... | collective-permute-start | bytes 4325384 | tf_op jit(solution)/shard_map/ppermute | solution.py:372
  418.5 4.8 collective-permute-start.4
  427.5 3.4 collective-permute-start.5
  438.5 82.4 %reduce-scatter.13.cloned.1.call-start = ((), (), s32[]{:S(2)}) async-start(), calls=%async_computation.17 | async-start | bytes 1310720 | tf_op jit(solution)/shard_map/reduce_scatter | solution.py:368
  491.3 107.1 %all-gather.20.cloned.1.call-start = ((), (), s32[]{:S(2)}) async-start(), calls=%async_computation.21 | async-start | bytes 4456448 | tf_op jit(solution)/shard_map/all_gather | solution.py:347
  520.9 303.5 %reduce-scatter.15.cloned.1.call-start = ((), (), s32[]{:S(2)}) async-start(), calls=%async_computation.18 | async-start | bytes 5242880 | tf_op jit(solution)/shard_map/reduce_scatter | solution.py:62
  639.4 1.6 collective-permute-start.6
  651.9 2.6 collective-permute-start.7
  660.7 173.2 %reduce-scatter.9.cloned.1.call-start = ((), (), s32[]{:S(2)}) async-start(), calls=%async_computation.13 | async-start | bytes 4456448 | tf_op jit(solution)/shard_map/reduce_scatter | solution.py:361
  661.8 2.2 collective-permute-start.3
  691.3 44.9 %all-to-all-start.3 = ((bf16[4,256,704]{1,2,0:T(8,128)(2,1)}), bf16[4,256,704]{1,2,0:T(8,128)(2,1)S(1)}, u32[]{:S(2)}, u32[]{:S(2)}) async-start(bf16[4,256,704]{1,2,0:T(8,128)(2,1)} %bitcast.133), calls=%async_computation.9 | async-start | bytes 2883584 | tf_op jit(solution)/shard_map/all_to_all | solution.py:382
  770.9 54.2 %copy-start.79 = (f32[2,1,64]{2,1,0:T(1,128)S(1)}, f32[2,1,64]{2,1,0:T(1,128)}, u32[]{:S(2)}) copy-start(f32[2,1,64]{2,1,0:T(1,128)} %param.25) | copy-start | bytes 1540
  771.0 54.2 %copy-start.80 = (f32[2,1,64]{2,1,0:T(1,128)S(1)}, f32[2,1,64]{2,1,0:T(1,128)}, u32[]{:S(2)}) copy-start(f32[2,1,64]{2,1,0:T(1,128)} %param.35) | copy-start | bytes 1540
  771.0 54.2 %copy-start.81 = (f32[2,1,64]{2,1,0:T(1,128)S(1)}, f32[2,1,64]{2,1,0:T(1,128)}, u32[]{:S(2)}) copy-start(f32[2,1,64]{2,1,0:T(1,128)} %param.34) | copy-start | bytes 1540
  777.0 48.8 %all-to-all-start.2 = ((bf16[4,256,256]{2,1,0:T(8,128)(2,1)}), bf16[4,256,256]{2,1,0:T(8,128)(2,1)S(1)}, u32[]{:S(2)}, u32[]{:S(2)}) async-start(bf16[4,256,256]{2,1,0:T(8,128)(2,1)} %bitcast.26), calls=%async_computation.8 | async-start | bytes 1048576 | tf_op jit(solution)/shard_map/all_to_all | solution.py:382
  780.4 71.1 %reduce-scatter.17.cloned.1.call-start = ((), (), s32[]{:S(2)}) async-start(), calls=%async_computation.19 | async-start | bytes 1310720 | tf_op jit(solution)/shard_map/reduce_scatter | solution.py:368
  827.4 24.2 %copy-start.44 = (bf16[512,256]{1,0:T(8,128)(2,1)S(1)}, bf16[512,256]{1,0:T(8,128)(2,1)}, u32[]{:S(2)}) copy-start(bf16[512,256]{1,0:T(8,128)(2,1)} %reduce-scatter.13.cloned.1.call-done) | copy-start | bytes 786436
  (76 other events, 343.0 us)
Sparse Core Ops, SparseCore 0:
  10.8 84.4 all-gather.17
  153.4 93.7 reduce-scatter.6
  249.3 27.5 all-gather.9
  278.3 27.4 all-gather.13
  307.4 52.0 all-gather.11
  361.2 52.5 all-gather.15
  438.6 52.6 reduce-scatter.10
  493.7 27.0 reduce-scatter.12
  523.6 74.7 all-gather.19
  660.8 51.2 reduce-scatter.14
  714.5 96.0 reduce-scatter.8
  824.5 26.9 reduce-scatter.16

commit v2 on v1

--- a/solution.py
+++ b/solution.py
@@ -341,26 +341,8 @@
     )
 
 
-def gather_joint(block):
-    places = lax.axis_size("dp"), lax.axis_size("col")
-    rows, columns = block.shape
-    parts = lax.all_gather(block, ("dp", "col"), axis=0, tiled=False)
-    parts = parts.reshape(places + (rows, columns)).transpose(0, 2, 1, 3)
-    return parts.reshape(places[0] * rows, places[1] * columns)
-
-
 def gather_steps(block):
     return width_gather(lax.all_gather(block, "dp", axis=0, tiled=True))
-
-
-def scatter_joint(whole):
-    data, cols = lax.axis_size("dp"), lax.axis_size("col")
-    rows, columns = whole.shape[0] // data, whole.shape[1] // cols
-    parts = whole.reshape(data, rows, cols, columns).transpose(0, 2, 1, 3)
-    parts = parts.reshape(data * cols, rows, columns)
-    return lax.psum_scatter(parts, ("dp", "col"), scatter_dimension=0, tiled=False).astype(
-        jnp.float32
-    )
 
 
 def scatter_steps(whole):
@@ -473,7 +455,7 @@
     units = w_down.shape[1]
     own = units // 2
 
-    whole_in = gather_joint(inputs)
+    whole_in = gather_steps(inputs)
     low_qkv = w_qkv[0, :, 0, :].astype(low_type)
     query_part = low_qkv[:, : GQ * HD].reshape(my_rows, data_count, 2 * HD).transpose(1, 0, 2)
     pair_part = jnp.broadcast_to(low_qkv[None, :, GQ * HD :], (data_count, my_rows, 2 * HD))
@@ -490,7 +472,8 @@
         .transpose(2, 0, 3, 1, 4)
         .reshape(data_count * my_rows, 4 * own)
     )
-    whole_cot = gather_steps(cotangent)
+    late_cot, whole_in = lax.optimization_barrier((cotangent, whole_in))
+    whole_cot = gather_steps(late_cot)
     weight_out = w_out[0].astype(low_type)
     weight_down = w_down[0].astype(low_type)
 
@@ -506,12 +489,13 @@
     cosine, sine = rope_tables(0, tokens, tokens)
     cosine, sine = cosine[:, 0], sine[:, 0]
     queries = rotate(mixed[:, :HD], cosine, sine).astype(low_type)
+    queries, weight_gate_up = lax.optimization_barrier((queries, weight_gate_up))
     keys = rotate(mixed[:, HD : 2 * HD], cosine, sine).astype(low_type)
     values = mixed[:, 2 * HD :].astype(low_type)
     attended, kept = attend(queries, keys, values, segments, count)
-    low_attended = attended.astype(low_type)
+    low_attended, whole_cot = lax.optimization_barrier((attended.astype(low_type), whole_cot))
     heads = in_order(is_first, low_attended, swap(low_attended))
-    middle = inputs.astype(jnp.float32) + scatter_joint(dot(heads, weight_out).astype(low_type))
+    middle = inputs.astype(jnp.float32) + scatter_steps(dot(heads, weight_out).astype(low_type))
     whole_middle = gather_steps(middle.astype(low_type)).astype(jnp.float32)
     scale_two = lax.rsqrt(
         row_total(jnp.sum(whole_middle * whole_middle, axis=1)) / D + NORM_EPS
@@ -529,8 +513,6 @@
     swish = gate * sigma
     low_hidden = (swish * up_value).astype(low_type)
     hidden = in_order(is_first, low_hidden, swap(low_hidden))
-    down = scatter_joint(dot(hidden, weight_down).astype(low_type))
-    layer_output = (middle + down).astype(low_type)
 
     mine_down = lax.dynamic_slice_in_dim(weight_down, row_place * own, own, 0)
     their_down = lax.dynamic_slice_in_dim(weight_down, (1 - row_place) * own, own, 0)
@@ -542,8 +524,13 @@
     unit_grads = jnp.concatenate([gate_grad, up_grad], axis=1).astype(low_type)
     unit_grads = in_order(is_first, unit_grads, swap(unit_grads))
     normed_two_grad = scatter_steps(dot_columns(unit_grads, weight_gate_up).astype(low_type))
-    grad_gate_up = dot_rows(normed_two, unit_grads).astype(low_type)
-    whole_grad = gather_joint(normed_two_grad.astype(low_type)).astype(jnp.float32)
+    grad_gate_up = exchange(dot_rows(normed_two, unit_grads).astype(low_type))
+    whole_grad = gather_steps(normed_two_grad.astype(low_type))
+    down_part = dot(hidden, weight_down).astype(low_type)
+    down_part, whole_grad = lax.optimization_barrier((down_part, whole_grad))
+    whole_grad = whole_grad.astype(jnp.float32)
+    down = scatter_steps(down_part)
+    layer_output = (middle + down).astype(low_type)
     total_two = row_total(jnp.sum(whole_grad * gain_two[None, :] * whole_middle, axis=1))
     shrink_two = scale_two * scale_two * scale_two * total_two / D
     branch_in = (
@@ -551,6 +538,7 @@
         + scale_two[:, None] * (whole_grad * gain_two[None, :])
         - whole_middle * shrink_two[:, None]
     ).astype(low_type)
+    branch_in, grad_gate_up = lax.optimization_barrier((branch_in, grad_gate_up))
     gain_two_grad = jnp.sum(whole_grad * whole_middle * scale_two[:, None], axis=0)
 
     def my_tokens(stat):
@@ -583,6 +571,7 @@
         ],
         axis=1,
     )
+    mixed_grad, layer_output = lax.optimization_barrier((mixed_grad, layer_output))
     part_one = dot_columns(mixed_grad, weight_qkv)
     normed_one_grad = scatter_steps(part_one.astype(low_type))
     grad_qkv = dot_rows(normed_one, mixed_grad).astype(low_type)
@@ -610,8 +599,7 @@
         ]
     )[:, None, :]
     gate_up_sum = (
-        exchange(grad_gate_up)
-        .reshape(data_count, my_rows, 2, 2, own)
+        grad_gate_up.reshape(data_count, my_rows, 2, 2, own)
         .transpose(1, 3, 0, 2, 4)
         .reshape(1, my_rows, 2, data_count * units)
         .astype(jnp.float32)

time: 868 us -> 842 us (0.970)
  local copies, waits for them, and re-layouts: 110 us -> 66.6 us
  waiting for transfers between devices: 447 us -> 485 us
  blocking collectives: 110 us -> 96.4 us
  other arithmetic: 81.1 us -> 71.4 us
    reduce_scatter x2 -> x0, waiting for transfers between devices: 93.8 us -> none  [scatter_joint(): lax.psum_scatter(parts, ('dp', 'col'), scatter_dimension=0, tiled=False)]
    all_gather x2 -> x0, waiting for transfers between devices: 89.8 us -> none  [gather_joint(): parts = lax.all_gather(block, ('dp', 'col'), axis=0, tiled=False)]
    reduce_scatter x2 -> x4, waiting for transfers between devices: 52.8 us -> 131 us  [column_scatter(): return lax.psum_scatter(values, 'col', scatter_dimension=1, tiled=True)]
    reduce_scatter x2 -> x4, waiting for transfers between devices: 47.2 us -> 103 us  [scatter_steps(): lax.psum_scatter(part, 'dp', scatter_dimension=0, tiled=True)]
    all_gather x2 -> x4, waiting for transfers between devices: 56.1 us -> 109 us  [gather_steps(): return width_gather(lax.all_gather(block, 'dp', axis=0, tiled=True))]
    all_gather x2 -> x4, waiting for transfers between devices: 42.3 us -> 92.6 us  [width_gather(): return lax.all_gather(values, 'col', axis=1, tiled=True)]
    reshape x2 -> x0, local copies, waits for them, and re-layouts: 15.9 us -> none  [scatter_joint(): parts = whole.reshape(data, rows, cols, columns).transpose(0, 2, 1, 3)]
    all_to_all x4, waiting for transfers between devices: 53.7 us -> 38 us  [exchange(): return lax.all_to_all(values, 'dp', split_axis=0, concat_axis=0, tiled=True)]
  transfers between devices with their start and end apart: 24 -> 28, of which waited for: 17 -> 21; matrix products, arithmetic and copies ran while one was open for 17% -> 21% of each run, Pallas kernels for 0% -> 0%
where the time goes in v2:
time: 842 us; the launch traced here: 833 us
  waiting for transfers between devices  485 us (58%)
  blocking collectives  96.4 us (11%)
  matrix products  79.5 us (9%)
  other arithmetic  71.4 us (8%)
  local copies, waits for them, and re-layouts  66.6 us (8%)
  starting transfers between devices  17.8 us (2%)
  between operations  15.8 us (2%)
    reduce_scatter x4, waiting for transfers between devices, column_scatter(): return lax.psum_scatter(values, 'col', scatter_dimension=1, tiled=True)  131 us
    all_gather x4, waiting for transfers between devices, gather_steps(): return width_gather(lax.all_gather(block, 'dp', axis=0, tiled=True))  109 us
    reduce_scatter x4, waiting for transfers between devices, scatter_steps(): lax.psum_scatter(part, 'dp', scatter_dimension=0, tiled=True)  103 us
    all_gather x4, waiting for transfers between devices, width_gather(): return lax.all_gather(values, 'col', axis=1, tiled=True)  92.6 us
    all_gather x1, blocking collectives, body_units(): lax.all_gather(gains[:, 0, :].astype(low_type), ('col', 'dp'), axis=1, ti...  46.7 us
    unnamed x168, local copies, waits for them, and re-layouts  46.7 us
    psum x1, blocking collectives, body_units(): lax.psum(jnp.concatenate([token_part, gain_part]), ('dp', 'row', 'col'))  40.7 us
    all_to_all x4, waiting for transfers between devices, exchange(): return lax.all_to_all(values, 'dp', split_axis=0, concat_axis=0, tiled=True)  38 us
  transfers between devices with their start and end apart: 28, of which 21 were waited for; matrix products, arithmetic and copies ran while one was open for 21% of the time, Pallas kernels for 0%

profile of v2, /device:TPU:0, one launch (start us, length us, event | category | flops | bytes accessed | tf_op | source)
XLA Modules:
  0.0 832.5 jit_solution(9543597047549234295)
XLA Ops:
  8.0 32.3 %all-gather.10.cloned.1.call-done = bf16[2048,256]{1,0:T(8,128)(2,1)} async-done(((bf16[512,256]{1,0:T(8,128)(2,1)}), bf16[2048,256]{1,0:T(8,128)(2,1)}) %all-gather.10.cloned.1.call-update) | async-done | bytes 1048592 | tf_op jit(solution)/shard_map/all_gather | solution.py:345
  52.5 46.7 %all-gather = bf16[2,1,1024]{1,0,2:T(2,128)(2,1)S(1)} all-gather(bf16[2,1,64]{1,0,2:T(2,128)(2,1)S(1)} %copy.119), channel_id=2, replica_groups=mesh['dp'=4,'row'=2,'col'=4] {'col','dp'}, dimensions={2}, use_global_device_ids=true | all-gather | bytes 4352 | tf_op jit(solution)/shard_map/all_gather | solution.py:465
  102.2 5.7 fusion.168
  125.4 12.8 %all-to-all-done.1 = bf16[4,256,704]{1,2,0:T(8,128)(2,1)S(1)} async-done(((bf16[4,256,704]{1,2,0:T(8,128)(2,1)}), bf16[4,256,704]{1,2,0:T(8,128)(2,1)S(1)}, u32[]{:S(2)}, u32[]{:S(2)}) %all-to-all-start.1) | async-done | bytes 1441824 | tf_op jit(solution)/shard_map/all_to_all | solution.py:364
  143.7 22.3 %all-gather.14.cloned.1.call-done = bf16[2048,256]{1,0:T(8,128)(2,1)} async-done(((bf16[512,256]{1,0:T(8,128)(2,1)}), bf16[2048,256]{1,0:T(8,128)(2,1)}) %all-gather.14.cloned.1.call-update) | async-done | bytes 1048592 | tf_op jit(solution)/shard_map/all_gather | solution.py:345
  185.4 34.4 %all-gather.16.cloned.1.call-done = bf16[2048,1024]{1,0:T(8,128)(2,1)} async-done(((bf16[2048,256]{1,0:T(8,128)(2,1)}), bf16[2048,1024]{1,0:T(8,128)(2,1)}) %all-gather.16.cloned.1.call-update) | async-done | bytes 4194320 | tf_op jit(solution)/shard_map/all_gather | solution.py:58
  227.7 52.8 %reduce-scatter.9.cloned.1.call-done = bf16[2048,256]{1,0:T(8,128)(2,1)} async-done(((bf16[2048,1024]{1,0:T(8,128)(2,1)}), bf16[2048,256]{1,0:T(8,128)(2,1)}) %reduce-scatter.9.cloned.1.call-update) | async-done | bytes 1048592 | tf_op jit(solution)/shard_map/reduce_scatter | solution.py:62
  280.5 29.3 %reduce-scatter.11.cloned.1.call-done = bf16[512,256]{1,0:T(8,128)(2,1)} async-done(((bf16[2048,256]{1,0:T(8,128)(2,1)}), bf16[512,256]{1,0:T(8,128)(2,1)}) %reduce-scatter.11.cloned.1.call-update) | async-done | bytes 262160 | tf_op jit(solution)/shard_map/reduce_scatter | solution.py:350
  311.7 27.0 %all-gather.18.cloned.1.call-done = bf16[2048,256]{1,0:T(8,128)(2,1)} async-done(((bf16[512,256]{1,0:T(8,128)(2,1)}), bf16[2048,256]{1,0:T(8,128)(2,1)}) %all-gather.18.cloned.1.call-update) | async-done | bytes 1048592 | tf_op jit(solution)/shard_map/all_gather | solution.py:345
  339.1 53.4 %all-gather.20.cloned.1.call-done = bf16[2048,1024]{1,0:T(8,128)(2,1)} async-done(((bf16[2048,256]{1,0:T(8,128)(2,1)}), bf16[2048,1024]{1,0:T(8,128)(2,1)}) %all-gather.20.cloned.1.call-update) | async-done | bytes 4194320 | tf_op jit(solution)/shard_map/all_gather | solution.py:58
  399.4 5.2 convolution_convert_fusion.3
  426.7 5.0 convolution_convert_fusion
  431.8 52.8 %reduce-scatter.13.cloned.1.call-done = bf16[2048,256]{1,0:T(8,128)(2,1)} async-done(((bf16[2048,1024]{1,0:T(8,128)(2,1)}), bf16[2048,256]{1,0:T(8,128)(2,1)}) %reduce-scatter.13.cloned.1.call-update) | async-done | bytes 1048592 | tf_op jit(solution)/shard_map/reduce_scatter | solution.py:62
  484.6 29.3 %reduce-scatter.15.cloned.1.call-done = bf16[512,256]{1,0:T(8,128)(2,1)} async-done(((bf16[2048,256]{1,0:T(8,128)(2,1)}), bf16[512,256]{1,0:T(8,128)(2,1)}) %reduce-scatter.15.cloned.1.call-update) | async-done | bytes 262160 | tf_op jit(solution)/shard_map/reduce_scatter | solution.py:350
  514.2 28.0 %all-gather.22.cloned.1.call-done = bf16[2048,256]{1,0:T(8,128)(2,1)} async-done(((bf16[512,256]{1,0:T(8,128)(2,1)}), bf16[2048,256]{1,0:T(8,128)(2,1)}) %all-gather.22.cloned.1.call-update) | async-done | bytes 1048592 | tf_op jit(solution)/shard_map/all_gather | solution.py:345
  542.2 6.3 fusion.25
  563.3 25.1 %all-to-all-done.2 = bf16[4,256,704]{1,2,0:T(8,128)(2,1)} async-done(((bf16[4,256,704]{1,2,0:T(8,128)(2,1)}), bf16[4,256,704]{1,2,0:T(8,128)(2,1)}, u32[]{:S(2)}, u32[]{:S(2)}) %all-to-all-start.2) | async-done | bytes 1441824 | tf_op jit(solution)/shard_map/all_to_all | solution.py:364
  596.0 6.1 fusion.12
  606.3 6.2 fusion.3
  626.6 25.0 %reduce-scatter.17.cloned.1.call-done = bf16[2048,256]{1,0:T(8,128)(2,1)} async-done(((bf16[2048,1024]{1,0:T(8,128)(2,1)}), bf16[2048,256]{1,0:T(8,128)(2,1)}) %reduce-scatter.17.cloned.1.call-update) | async-done | bytes 1048592 | tf_op jit(solution)/shard_map/reduce_scatter | solution.py:62
  654.8 26.2 %reduce-scatter.19.cloned.1.call-done = bf16[512,256]{1,0:T(8,128)(2,1)} async-done(((bf16[2048,256]{1,0:T(8,128)(2,1)}), bf16[512,256]{1,0:T(8,128)(2,1)}) %reduce-scatter.19.cloned.1.call-update) | async-done | bytes 262160 | tf_op jit(solution)/shard_map/reduce_scatter | solution.py:350
  682.8 5.8 multiply_reduce_fusion.1
  694.1 5.7 copy.132
  701.7 8.3 multiply_subtract_fusion.1
  716.0 5.7 copy.135
  721.7 6.4 multiply_subtract_fusion
  728.1 5.5 copy.136
  733.6 5.7 copy.137
  743.1 5.1 multiply_subtract_fusion.3
  755.5 40.7 %psum.31 = f32[4096]{0:T(1024)S(1)} all-reduce(f32[4096]{0:T(1024)S(1)} %pad_maximum_fusion.27), channel_id=1, replica_groups=mesh['dp'=4,'row'=2,'col'=4] {'dp','row','col'}, use_global_device_ids=true, to_apply=%region_25.26 | all-reduce | flops 4096 | bytes 32768 | tf_op jit(solution)/shard_map/psum | solution.py:586
  799.6 6.1 multiply_subtract_fusion.2
  805.6 17.8 %reduce-scatter.23.cloned.1.call-done = bf16[512,256]{1,0:T(8,128)(2,1)} async-done(((bf16[2048,256]{1,0:T(8,128)(2,1)}), bf16[512,256]{1,0:T(8,128)(2,1)}) %reduce-scatter.23.cloned.1.call-update) | async-done | bytes 262160 | tf_op jit(solution)/shard_map/reduce_scatter | solution.py:350
  (342 shorter events, 171.9 us)
Async XLA Ops:
  7.2 33.1 %all-gather.10.cloned.1.call-start = ((), (), s32[]{:S(2)}) async-start(), calls=%async_computation.12 | async-start | bytes 1310720 | tf_op jit(solution)/shard_map/all_gather | solution.py:345
  7.9 105.7 %all-gather.12.cloned.1.call-start = ((), (), s32[]{:S(2)}) async-start(), calls=%async_computation.13 | async-start | bytes 5242880 | tf_op jit(solution)/shard_map/all_gather | solution.py:58
  42.5 65.3 %all-to-all-start = ((bf16[4,256,256]{1,2,0:T(8,128)(2,1)}), bf16[4,256,256]{1,2,0:T(8,128)(2,1)S(1)}, u32[]{:S(2)}, u32[]{:S(2)}) async-start(bf16[4,256,256]{1,2,0:T(8,128)(2,1)} %pad_maximum_fusion.14), calls=%async_computation | async-start | bytes 1048576 | tf_op jit(solution)/shard_map/all_to_all | solution.py:364
  52.5 59.5 %copy-start.58 = (s32[2048]{0:T(1024)S(1)}, s32[2048]{0:T(1024)}, u32[]{:S(2)}) copy-start(s32[2048]{0:T(1024)} %param.19) | copy-start | bytes 24580
  107.8 30.3 %all-to-all-start.1 = ((bf16[4,256,704]{1,2,0:T(8,128)(2,1)}), bf16[4,256,704]{1,2,0:T(8,128)(2,1)S(1)}, u32[]{:S(2)}, u32[]{:S(2)}) async-start(bf16[4,256,704]{1,2,0:T(8,128)(2,1)} %bitcast.104), calls=%async_computation.1 | async-start | bytes 2883584 | tf_op jit(solution)/shard_map/all_to_all | solution.py:364
  111.4 54.6 %all-gather.14.cloned.1.call-start = ((), (), s32[]{:S(2)}) async-start(), calls=%async_computation.14 | async-start | bytes 1310720 | tf_op jit(solution)/shard_map/all_gather | solution.py:345
  124.1 16.6 %collective-permute-start = (bf16[2048,192]{0,1:T(8,128)(2,1)}, bf16[2048,192]{0,1:T(8,128)(2,1)}, u32[]{:S(2)}, u32[]{:S(2)}) collective-permute-start(bf16[2048,192]{0,1:T(8,128)(2,1)} %pad_maximum_fusion.10), channel_id=1, source_target_pairs={{0,4},{4,0},{1,5},{5,1},{2,6},{6,2},{3,7},{7,3},{8,12},{12,8},{9,1... | collective-permute-start | bytes 2359304 | tf_op jit(solution)/shard_map/ppermute | solution.py:354
  140.6 79.2 %all-gather.16.cloned.1.call-start = ((), (), s32[]{:S(2)}) async-start(), calls=%async_computation.15 | async-start | bytes 5242880 | tf_op jit(solution)/shard_map/all_gather | solution.py:58
  166.0 114.5 %reduce-scatter.9.cloned.1.call-start = ((), (), s32[]{:S(2)}) async-start(), calls=%async_computation.16 | async-start | bytes 5242880 | tf_op jit(solution)/shard_map/reduce_scatter | solution.py:62
  219.7 1.7 collective-permute-start.1
  227.6 82.3 %copy-start.18 = (bf16[512,256]{1,0:T(8,128)(2,1)S(1)}, bf16[512,256]{1,0:T(8,128)(2,1)}, u32[]{:S(2)}) copy-start(bf16[512,256]{1,0:T(8,128)(2,1)} %param.18) | copy-start | bytes 786436
  227.6 82.2 %reduce-scatter.11.cloned.1.call-start = ((), (), s32[]{:S(2)}) async-start(), calls=%async_computation.17 | async-start | bytes 1310720 | tf_op jit(solution)/shard_map/reduce_scatter | solution.py:350
  280.5 58.1 %all-gather.18.cloned.1.call-start = ((), (), s32[]{:S(2)}) async-start(), calls=%async_computation.18 | async-start | bytes 1310720 | tf_op jit(solution)/shard_map/all_gather | solution.py:345
  311.6 80.9 %all-gather.20.cloned.1.call-start = ((), (), s32[]{:S(2)}) async-start(), calls=%async_computation.19 | async-start | bytes 5242880 | tf_op jit(solution)/shard_map/all_gather | solution.py:58
  338.7 145.9 %reduce-scatter.13.cloned.1.call-start = ((), (), s32[]{:S(2)}) async-start(), calls=%async_computation.20 | async-start | bytes 5242880 | tf_op jit(solution)/shard_map/reduce_scatter | solution.py:62
  404.7 7.5 collective-permute-start.2
  411.8 5.2 collective-permute-start.4
  421.1 3.3 collective-permute-start.5
  431.7 82.2 %reduce-scatter.15.cloned.1.call-start = ((), (), s32[]{:S(2)}) async-start(), calls=%async_computation.21 | async-start | bytes 1310720 | tf_op jit(solution)/shard_map/reduce_scatter | solution.py:350
  484.6 57.6 %all-gather.22.cloned.1.call-start = ((), (), s32[]{:S(2)}) async-start(), calls=%async_computation.22 | async-start | bytes 1310720 | tf_op jit(solution)/shard_map/all_gather | solution.py:345
  514.0 81.9 %all-gather.24.cloned.1.call-start = ((), (), s32[]{:S(2)}) async-start(), calls=%async_computation.23 | async-start | bytes 5242880 | tf_op jit(solution)/shard_map/all_gather | solution.py:58
  549.7 38.7 %all-to-all-start.2 = ((bf16[4,256,704]{1,2,0:T(8,128)(2,1)}), bf16[4,256,704]{1,2,0:T(8,128)(2,1)}, u32[]{:S(2)}, u32[]{:S(2)}) async-start(bf16[4,256,704]{1,2,0:T(8,128)(2,1)} %bitcast.106), calls=%async_computation.6 | async-start | bytes 2883584 | tf_op jit(solution)/shard_map/all_to_all | solution.py:364
  554.1 97.5 %reduce-scatter.17.cloned.1.call-start = ((), (), s32[]{:S(2)}) async-start(), calls=%async_computation.24 | async-start | bytes 5242880 | tf_op jit(solution)/shard_map/reduce_scatter | solution.py:62
  554.1 2.5 collective-permute-start.3
  596.0 85.0 %reduce-scatter.19.cloned.1.call-start = ((), (), s32[]{:S(2)}) async-start(), calls=%async_computation.25 | async-start | bytes 1310720 | tf_op jit(solution)/shard_map/reduce_scatter | solution.py:350
  614.8 1.6 collective-permute-start.6
  651.6 144.5 %reduce-scatter.21.cloned.1.call-start = ((), (), s32[]{:S(2)}) async-start(), calls=%async_computation.26 | async-start | bytes 5242880 | tf_op jit(solution)/shard_map/reduce_scatter | solution.py:62
  652.0 2.4 collective-permute-start.7
  748.2 48.7 %copy-start.77 = (f32[2,1,64]{2,1,0:T(1,128)S(1)}, f32[2,1,64]{2,1,0:T(1,128)}, u32[]{:S(2)}) copy-start(f32[2,1,64]{2,1,0:T(1,128)} %param.25) | copy-start | bytes 1540
  748.2 48.7 %copy-start.78 = (f32[2,1,64]{2,1,0:T(1,128)S(1)}, f32[2,1,64]{2,1,0:T(1,128)}, u32[]{:S(2)}) copy-start(f32[2,1,64]{2,1,0:T(1,128)} %param.35) | copy-start | bytes 1540
  751.0 46.5 %all-to-all-start.3 = ((bf16[4,256,256]{2,1,0:T(8,128)(2,1)}), bf16[4,256,256]{2,1,0:T(8,128)(2,1)S(1)}, u32[]{:S(2)}, u32[]{:S(2)}) async-start(bf16[4,256,256]{2,1,0:T(8,128)(2,1)} %bitcast.12), calls=%async_computation.11 | async-start | bytes 1048576 | tf_op jit(solution)/shard_map/all_to_all | solution.py:364
  754.5 68.9 %reduce-scatter.23.cloned.1.call-start = ((), (), s32[]{:S(2)}) async-start(), calls=%async_computation.27 | async-start | bytes 1310720 | tf_op jit(solution)/shard_map/reduce_scatter | solution.py:350
  (76 other events, 705.3 us)
Sparse Core Ops, SparseCore 0:
  9.6 30.6 all-gather.9
  42.1 56.9 all-gather.11
  140.7 25.2 all-gather.13
  167.7 52.0 all-gather.15
  227.8 52.6 reduce-scatter.8
  282.7 27.0 reduce-scatter.10
  312.0 26.5 all-gather.17
  340.5 52.0 all-gather.19
  431.9 52.6 reduce-scatter.12
  486.8 27.0 reduce-scatter.14
  515.5 26.5 all-gather.21
  543.8 52.0 all-gather.23
  598.9 52.6 reduce-scatter.16
  653.9 27.0 reduce-scatter.18
  688.7 51.3 reduce-scatter.20
  796.3 27.0 reduce-scatter.22
